TPU v7x, 512 devices: a whole 4x8x8 slice. The times are simulated.
512 devices in a mesh: rep: 32 (over y_lo, z), ctx: 16 (over y_hi, x, core).
Axes of the slice: x: 4, y: 8 (y_hi: 2, y_lo: 4; y = y_hi * 4 + y_lo), z: 8, core: 2. Of those that a mesh axis runs over, the one named last changes fastest.
Arguments:
- q_first: bfloat16 [64, 4096], P('rep'), as said below
- kv_first: bfloat16 [64, 1024], P('rep'), as said below
- hidden_next: bfloat16 [64, 5120], P('rep', 'ctx'), as said below
- lengths: int32 [64], P('rep'), may hold values from 4096 to 16384, as said below
- owners: int32 [16, 32], P('ctx'), may hold values from 0 to 31, as said below
- sectioned: bfloat16 [32, 160, 5120], P('rep', 'ctx'), as said below
- kv_cache: bfloat16 [64, 2, 16384, 512], P('rep', None, 'ctx'), as said below
Outputs:
- attended: bfloat16 [64, 2, 4096], P('rep')
- kv_second: bfloat16 [64, 1024], P('rep')
Inputs may be any that keep to these rules, and one draw needn't show every extreme that they name: `q_first`: queries of the first step. `kv_first`: key and value of the first step's token. `hidden_next`: input rows of the second step. `lengths`: some rollout uses all 16384 positions. Each row of owners is a permutation of the 32 replica slots. `sectioned`: projection rows. `kv_cache`: cached keys and values.
All inputs are finite; a program needn't handle non-finite values.
Results may differ from a plain program's by a relative error of at most 0.007.
Values may be sent and summed in bfloat16 or wider, within the bound.
No kernel may reach another device: no remote copies, remote signals or barrier semaphores. Data moves between devices by JAX's collectives and lax.ppermute only.
A program may use at most 64 MiB of HBM per device.

v0:
```python
import jax
import jax.numpy as jnp
from jax import lax
from jax.sharding import PartitionSpec as P

HD = 128
QH = 32
KVH = 4


def joined(value, axis, join):
    pieces = jax.tree.map(lambda part: lax.all_gather(part, axis), value)
    head = jax.tree.map(lambda part: part[0], pieces)
    tail = jax.tree.map(lambda part: part[1:], pieces)
    so_far, _ = lax.scan(lambda so_far, share: (join(so_far, share), None), head, tail)
    return so_far


def rotate_pairs(vectors, position):
    halfway = vectors.shape[-1] // 2
    frequency = jnp.power(
        jnp.float32(1000000.0), -(jnp.arange(halfway, dtype=jnp.float32) * 2.0 / vectors.shape[-1])
    )
    angles = position * frequency
    cosine = jnp.cos(angles)
    sine_value = jnp.sin(angles)
    first_half = vectors[..., :halfway]
    second_half = vectors[..., halfway:]
    return jnp.concatenate(
        [
            first_half * cosine - second_half * sine_value,
            second_half * cosine + first_half * sine_value,
        ],
        axis=-1,
    )


def split_heads(queries):
    row_count, step_count, head_count, head_size = queries.shape
    groups = head_count // KVH
    arranged = queries.reshape(row_count, step_count, KVH, groups, head_size).transpose(
        0, 2, 1, 3, 4
    )
    return arranged.reshape(row_count, KVH, step_count * groups, head_size)


def local_part(grouped, cache_keys, cache_values, usable):
    scores = jnp.einsum(
        "rgqd,rkgd->rgqk", grouped, cache_keys, preferred_element_type=jnp.float32
    ) * HD ** (-0.5)
    allowed = usable[:, None, None, :]
    masked = jnp.where(allowed, scores, -1e30)
    biggest = jnp.max(masked, axis=-1, keepdims=True)
    exponentials = jnp.where(allowed, jnp.exp(masked - biggest), 0.0)
    totals = jnp.sum(exponentials, axis=-1, keepdims=True)
    summed = jnp.einsum(
        "rgqk,rkgd->rgqd",
        exponentials.astype(jnp.bfloat16),
        cache_values,
        preferred_element_type=jnp.float32,
    )
    return (biggest, totals, summed)


def combine_parts(earlier, later):
    biggest = jnp.maximum(earlier[0], later[0])
    left_scale = jnp.exp(earlier[0] - biggest)
    right_scale = jnp.exp(later[0] - biggest)
    return (
        biggest,
        earlier[1] * left_scale + later[1] * right_scale,
        earlier[2] * left_scale + later[2] * right_scale,
    )


def finish(merged, grouped, new_keys, new_values):
    scores = jnp.einsum(
        "rgqd,rngd->rgqn", grouped, new_keys, preferred_element_type=jnp.float32
    ) * HD ** (-0.5)
    biggest = jnp.maximum(merged[0], jnp.max(scores, axis=-1, keepdims=True))
    carried = jnp.exp(merged[0] - biggest)
    exponentials = jnp.exp(scores - biggest)
    totals = merged[1] * carried + jnp.sum(exponentials, axis=-1, keepdims=True)
    summed = merged[2] * carried + jnp.einsum(
        "rgqn,rngd->rgqd",
        exponentials.astype(jnp.bfloat16),
        new_values,
        preferred_element_type=jnp.float32,
    )
    return (summed / totals).reshape(summed.shape[0], -1)


def local(q_first, kv_first, hidden_next, lengths, owners, sectioned, kv_cache):
    row_count = q_first.shape[0]
    width_q = QH * HD
    width_kv = KVH * HD
    local_ctx = kv_cache.shape[2]
    cache_keys = kv_cache[:, 0].reshape(row_count, local_ctx, KVH, HD)
    cache_values = kv_cache[:, 1].reshape(row_count, local_ctx, KVH, HD)
    position = lax.axis_index("ctx") * local_ctx + jnp.arange(local_ctx, dtype=jnp.int32)
    usable = position[None, :] < lengths[:, None]
    first_query = q_first.reshape(row_count, 1, QH, HD)
    first_key = kv_first[:, :width_kv].reshape(row_count, 1, KVH, HD)
    first_value = kv_first[:, width_kv:].reshape(row_count, 1, KVH, HD)
    replicas = lax.axis_size("rep")
    owner_row = owners[0]
    bucket_rows = sectioned.shape[1]
    first_grouped = split_heads(first_query)
    first_big, first_tot, first_sum = local_part(first_grouped, cache_keys, cache_values, usable)
    first_part = joined((first_big, first_tot, first_sum), "ctx", combine_parts)
    selector = (owner_row[None, :] == jnp.arange(replicas, dtype=jnp.int32)[:, None]).astype(
        jnp.bfloat16
    )
    by_bucket = hidden_next.reshape(row_count, replicas, bucket_rows)
    by_slot = jnp.einsum(
        "sb,rbi->rsi", selector, by_bucket, preferred_element_type=jnp.float32
    ).astype(jnp.bfloat16)
    partial_sum = jnp.einsum(
        "rsi,sic->rc",
        by_slot,
        lax.all_gather(sectioned, "rep", axis=0, tiled=True),
        preferred_element_type=jnp.float32,
    )
    projected = lax.psum(partial_sum, "ctx")
    rotation = (lengths + 1).astype(jnp.float32)[:, None, None]
    second_query = rotate_pairs(projected[:, :width_q].reshape(row_count, QH, HD), rotation).astype(
        jnp.bfloat16
    )
    second_key = rotate_pairs(
        projected[:, width_q : width_q + width_kv].reshape(row_count, KVH, HD), rotation
    ).astype(jnp.bfloat16)
    second_value = projected[:, width_q + width_kv :].astype(jnp.bfloat16)
    second_query, second_key, second_value = (second_query, second_key, second_value)
    second_grouped = split_heads(second_query[:, None])
    second_big, second_tot, second_sum = local_part(
        second_grouped, cache_keys, cache_values, usable
    )
    second_part = joined((second_big, second_tot, second_sum), "ctx", combine_parts)
    both_keys = jnp.concatenate([first_key, second_key[:, None]], axis=1)
    both_values = jnp.concatenate(
        [first_value, second_value.reshape(row_count, 1, KVH, HD)], axis=1
    )
    first_out = finish(first_part, first_grouped, first_key, first_value)
    second_out = finish(second_part, second_grouped, both_keys, both_values)
    attended = jnp.stack([first_out, second_out], axis=1).astype(jnp.bfloat16)
    kv_second = jnp.concatenate([second_key.reshape(row_count, width_kv), second_value], axis=1)
    return (attended, kv_second)


def solution(mesh):
    placed = (
        P("rep", None),
        P("rep", None),
        P("rep", "ctx"),
        P("rep"),
        P("ctx", None),
        P("rep", "ctx", None),
        P("rep", None, "ctx", None),
    )
    return jax.shard_map(
        local,
        mesh=mesh,
        in_specs=placed,
        out_specs=(P("rep", None, None), P("rep", None)),
        check_vma=False,
    )
```

profile of v0, /device:TPU:1, one launch (start us, length us, event | category | flops | bytes accessed | tf_op | source)
XLA Modules:
  0.0 385.7 jit_solution(14215941705321996914)
XLA Ops:
  7.2 0.7 all-gather.8.cloned.1.call-update
  7.9 0.7 slice_convert_fusion.1
  8.6 4.5 %fusion.64 = (bf16[2,1,1024,512]{3,2,1,0:T(8,128)(2,1)}, bf16[2,1,1024,512]{3,2,1,0:T(8,128)(2,1)}) fusion(bf16[2,2,1024,512]{3,2,1,0:T(8,128)(2,1)} %param.17), kind=kLoop, calls=%fused_computation.111 | loop fusion | bytes 8388608 | tf_op jit(solution)/shard_map/slice | solution.py:99
  13.1 3.0 copy.67
  16.2 4.0 %copy.66 = bf16[2,1,1024,512]{2,3,0,1:T(8,128)(2,1)} copy(bf16[2,1,1024,512]{3,2,1,0:T(8,128)(2,1)} %get-tuple-element.145) | data formatting | bytes 4194304
  20.2 2.1 fusion.66
  22.3 0.7 fusion.22
  23.0 36.3 %all-gather.2 = f32[32,4,8,128]{3,2,1,0:T(8,128)S(1)} all-gather(f32[2,4,8,128]{3,2,1,0:T(8,128)S(1)} %fusion.22), channel_id=4, replica_groups=mesh['rep'=32,'ctx'=16] {'ctx'}, dimensions={0}, use_global_device_ids=true | all-gather | bytes 557056 | tf_op jit(solution)/shard_map/all_gather | solution.py:12
  59.5 24.2 %all-gather = f32[32,4,8]{2,1,0:T(4,128)S(1)} all-gather(f32[2,4,8]{2,1,0:T(4,128)S(1)} %get-tuple-element.162), channel_id=2, replica_groups=mesh['rep'=32,'ctx'=16] {'ctx'}, dimensions={0}, use_global_device_ids=true | all-gather | bytes 4352 | tf_op jit(solution)/shard_map/all_gather | solution.py:12
  84.2 74.4 %all-gather.8.cloned.1.call-done = bf16[32,10,5120]{2,1,0:T(8,128)(2,1)} async-done(((bf16[1,10,5120]{2,1,0:T(8,128)(2,1)}), bf16[32,10,5120]{2,1,0:T(8,128)(2,1)}) %all-gather.8.cloned.1.call-update) | async-done | bytes 3276816 | tf_op jit(solution)/shard_map/all_gather | solution.py:121
  158.6 4.3 %convolution_bitcast_fusion = f32[2,5120]{1,0:T(2,128)S(1)} fusion(bf16[32,10,5120]{2,1,0:T(8,128)(2,1)} %all-gather.8.cloned.1.call-done, bf16[2,32,10]{1,2,0:T(8,128)(2,1)S(1)} %fusion.15), kind=kOutput, calls=%fused_computation.20 | convolution fusion | flops 6553600 | bytes 3319040 | tf_op jit(solution)/shard_map/rsi,sic->rc/dot_general | solution.py:118
  163.0 96.2 %psum.7 = f32[2,5120]{1,0:T(2,128)S(1)} all-reduce(f32[2,5120]{1,0:T(2,128)S(1)} %convolution_bitcast_fusion), channel_id=1, replica_groups=mesh['rep'=32,'ctx'=16] {'ctx'}, use_global_device_ids=true, to_apply=%region_4.5 | all-reduce | flops 10240 | bytes 81920 | tf_op jit(solution)/shard_map/psum | solution.py:124
  259.3 2.1 fusion.65
  261.5 0.2 fusion.17
  261.7 0.7 fusion.20
  262.4 32.3 %all-gather.1 = f32[32,4,8]{2,1,0:T(4,128)S(1)} all-gather(f32[2,4,8]{2,1,0:T(4,128)S(1)} %get-tuple-element.106), channel_id=3, replica_groups=mesh['rep'=32,'ctx'=16] {'ctx'}, dimensions={0}, use_global_device_ids=true | all-gather | bytes 4352 | tf_op jit(solution)/shard_map/all_gather | solution.py:12
  294.7 25.9 %all-gather.3 = f32[32,4,8]{2,1,0:T(4,128)S(1)} all-gather(f32[2,4,8]{2,1,0:T(4,128)S(1)} %get-tuple-element.160), channel_id=5, replica_groups=mesh['rep'=32,'ctx'=16] {'ctx'}, dimensions={0}, use_global_device_ids=true | all-gather | bytes 4352 | tf_op jit(solution)/shard_map/all_gather | solution.py:12
  320.6 24.2 %all-gather.4 = f32[32,4,8]{2,1,0:T(4,128)S(1)} all-gather(f32[2,4,8]{2,1,0:T(4,128)S(1)} %get-tuple-element.107), channel_id=6, replica_groups=mesh['rep'=32,'ctx'=16] {'ctx'}, dimensions={0}, use_global_device_ids=true | all-gather | bytes 4352 | tf_op jit(solution)/shard_map/all_gather | solution.py:12
  344.8 26.8 %all-gather.5 = f32[32,4,8,128]{3,2,1,0:T(8,128)S(1)} all-gather(f32[2,4,8,128]{3,2,1,0:T(8,128)S(1)} %fusion.20), channel_id=7, replica_groups=mesh['rep'=32,'ctx'=16] {'ctx'}, dimensions={0}, use_global_device_ids=true | all-gather | bytes 557056 | tf_op jit(solution)/shard_map/all_gather | solution.py:12
  371.9 0.6 pad_maximum_fusion.2
  372.5 2.5 while.28
  375.2 2.5 while.29
  377.7 0.2 fusion.67
  378.2 0.6 copy.58
  (180 shorter events, 5.5 us)
Async XLA Ops:
  7.2 151.5 %all-gather.8.cloned.1.call-start = ((), (), s32[]{:S(2)}) async-start(), calls=%async_computation | async-start | bytes 5406720 | tf_op jit(solution)/shard_map/all_gather | solution.py:121
  16.1 4.0 %copy-start.4 = (s32[2]{0:T(128)S(1)}, s32[2]{0:T(128)}, u32[]{:S(2)}) copy-start(s32[2]{0:T(128)} %param.14) | copy-start | bytes 28
  16.2 4.1 %copy-start.2 = (bf16[2,4096]{1,0:T(2,128)(2,1)S(1)}, bf16[2,4096]{1,0:T(2,128)(2,1)}, u32[]{:S(2)}) copy-start(bf16[2,4096]{1,0:T(2,128)(2,1)} %param.11) | copy-start | bytes 49156
  22.3 37.1 %copy-start.3 = (bf16[2,320]{1,0:T(2,128)(2,1)S(1)}, bf16[2,320]{1,0:T(2,128)(2,1)}, u32[]{:S(2)}) copy-start(bf16[2,320]{1,0:T(2,128)(2,1)} %param.13) | copy-start | bytes 3844
  22.3 61.7 %copy-start.5 = (s32[1,32]{1,0:T(1,128)S(1)}, s32[1,32]{1,0:T(1,128)}, u32[]{:S(2)}) copy-start(s32[1,32]{1,0:T(1,128)} %param.15) | copy-start | bytes 388
  83.8 177.7 %copy-start = (f32[32,4,8]{2,1,0:T(4,128)}, f32[32,4,8]{2,1,0:T(4,128)S(1)}, u32[]{:S(2)}) copy-start(f32[32,4,8]{2,1,0:T(4,128)S(1)} %all-gather) | copy-start | bytes 12292
  259.2 3.2 copy-start.1
  261.7 110.8 %slice-start = ((f32[32,4,8]{2,1,0:T(4,128)}), f32[30,4,8]{2,1,0:T(4,128)S(1)}, s32[]{:S(2)}) async-start(f32[32,4,8]{2,1,0:T(4,128)} %copy-done), calls=%async_computation.1 | async-start | bytes 122880 | tf_op jit(solution)/shard_map/slice | solution.py:14
  262.4 109.3 %slice-start.1 = ((f32[2,5120]{1,0:T(2,128)}), f32[2,512]{1,0:T(2,128)S(1)}, s32[]{:S(2)}) async-start(f32[2,5120]{1,0:T(2,128)} %copy-done.1), calls=%async_computation.2 | async-start | bytes 8192 | tf_op jit(solution)/shard_map/slice | solution.py:130
Sparse Core Ops, SparseCore 0:
  10.1 148.5 all-gather.7
where the time goes:
time: 386 us
  blocking collectives  266 us (69%)
  waiting for transfers between devices  75.1 us (19%)
  between operations  14.2 us (4%)
  local copies, waits for them, and re-layouts  12.6 us (3%)
  matrix products  10.6 us (3%)
  other arithmetic  6.03 us (2%)
    all_gather x6, blocking collectives, joined(): pieces = jax.tree.map(lambda part: lax.all_gather(part, axis), value)  170 us
    psum x1, blocking collectives, local(): projected = lax.psum(partial_sum, 'ctx')  96.2 us
    all_gather x1, waiting for transfers between devices, local(): lax.all_gather(sectioned, 'rep', axis=0, tiled=True)  74.4 us
  transfers between devices with their start and end apart: 1, of which 1 were waited for; matrix products, arithmetic and copies ran while one was open for 4% of the time, Pallas kernels for 0%

commit v1 on v0

v1 whole, which is shorter than its diff:
```python
import jax
import jax.numpy as jnp
from jax import lax
from jax.experimental import pallas as pl
from jax.experimental.pallas import tpu as pltpu
from jax.sharding import Mesh, PartitionSpec as P

HD = 128
QH = 32
KVH = 4
GROUP = QH // KVH
HEADS = QH + 2 * KVH
REP = ("yl", "z")
CHIPS = ("yh", "x")
CTX = ("yh", "x", "core")
MASKED = -1e30
VMEM_BYTES = 40 * 1024 * 1024


def spread(rows):
    return jnp.concatenate(
        [jnp.broadcast_to(rows[g : g + 1], (GROUP, HD)) for g in range(KVH)], axis=0
    )


def attend(query, halves, starts, length, extras):
    parts = []
    for (keys, _), start in zip(halves, starts):
        positions = keys.shape[0]
        scores = jnp.concatenate(
            [
                lax.dot_general(
                    query[g * GROUP : (g + 1) * GROUP],
                    keys[:, g * HD : (g + 1) * HD],
                    (((1,), (1,)), ((), ())),
                    preferred_element_type=jnp.float32,
                )
                for g in range(KVH)
            ],
            axis=0,
        ) * HD ** (-0.5)
        position = start + lax.broadcasted_iota(jnp.int32, (1, positions), 1)
        parts.append(jnp.where(position < length, scores, MASKED))
    wide = query.astype(jnp.float32)
    singles = []
    for key_rows, _, counted in extras:
        score = jnp.sum(wide * spread(key_rows.astype(jnp.float32)), axis=1, keepdims=True)
        singles.append(jnp.where(counted, score * HD ** (-0.5), MASKED))
    biggest = jnp.maximum(
        jnp.max(parts[0], axis=1, keepdims=True), jnp.max(parts[1], axis=1, keepdims=True)
    )
    for score in singles:
        biggest = jnp.maximum(biggest, score)
    total = jnp.zeros((QH, 1), jnp.float32)
    summed = jnp.zeros((QH, HD), jnp.float32)
    for part, (_, values) in zip(parts, halves):
        exponentials = jnp.where(part > 0.5 * MASKED, jnp.exp(part - biggest), 0.0)
        total += jnp.sum(exponentials, axis=1, keepdims=True)
        rounded = exponentials.astype(jnp.bfloat16)
        summed += jnp.concatenate(
            [
                jnp.dot(
                    rounded[g * GROUP : (g + 1) * GROUP],
                    values[:, g * HD : (g + 1) * HD],
                    preferred_element_type=jnp.float32,
                )
                for g in range(KVH)
            ],
            axis=0,
        )
    for score, (_, value_rows, _) in zip(singles, extras):
        exponential = jnp.where(score > 0.5 * MASKED, jnp.exp(score - biggest), 0.0)
        total += exponential
        rounded = exponential.astype(jnp.bfloat16).astype(jnp.float32)
        summed += rounded * spread(value_rows.astype(jnp.float32))
    used = total > 0.0
    safe = jnp.where(used, total, 1.0)
    return summed / safe, jnp.where(used, biggest + jnp.log(safe), MASKED)


def as_row(column):
    rows = column.shape[0]
    diagonal = lax.broadcasted_iota(jnp.int32, (rows, HD), 0) == lax.broadcasted_iota(
        jnp.int32, (rows, HD), 1
    )
    return jnp.sum(jnp.where(diagonal, column, 0.0), axis=0, keepdims=True)


def as_column(row, rows):
    diagonal = lax.broadcasted_iota(jnp.int32, (rows, HD), 0) == lax.broadcasted_iota(
        jnp.int32, (rows, HD), 1
    )
    return jnp.sum(jnp.where(diagonal, row, 0.0), axis=1, keepdims=True)


def pack(attended, weight):
    return jnp.concatenate(
        [attended, jnp.broadcast_to(as_row(weight), (8, HD))], axis=0
    )


def halves_of(own, other):
    return ((own.at[0, 0], own.at[0, 1]), (other.at[0], other.at[1]))


def first_kernel(scalars, query, fresh, own, other, out):
    counted = scalars[4] == 0
    attended, weight = attend(
        query[...],
        halves_of(own, other),
        (scalars[1], scalars[2]),
        scalars[3],
        ((fresh[0:KVH], fresh[KVH:], counted),),
    )
    out[...] = pack(attended, weight)


def second_kernel(scalars, shares, cosine, sine, fresh, own, other, out, made):
    counted = scalars[4] == 0
    projected = shares[0]
    for i in range(1, shares.shape[0]):
        projected += shares[i]
    turned = projected[: QH + KVH]
    turned = turned * cosine[...] + pltpu.roll(turned, HD // 2, 1) * sine[...]
    query = turned[:QH].astype(jnp.bfloat16)
    second = jnp.concatenate([turned[QH:], projected[QH + KVH :]], axis=0).astype(jnp.bfloat16)
    made[...] = second
    attended, weight = attend(
        query,
        halves_of(own, other),
        (scalars[1], scalars[2]),
        scalars[3],
        (
            (fresh[0:KVH], fresh[KVH:], counted),
            (second[0:KVH], second[KVH:], counted),
        ),
    )
    out[...] = pack(attended, weight)


def combine_kernel(shares, out):
    count = shares.shape[0]
    for step in range(2):
        weights = [
            as_column(shares[i, step, QH : QH + 1], QH) for i in range(count)
        ]
        biggest = weights[0]
        for weight in weights[1:]:
            biggest = jnp.maximum(biggest, weight)
        total = jnp.zeros((QH, 1), jnp.float32)
        summed = jnp.zeros((QH, HD), jnp.float32)
        for i in range(count):
            scale = jnp.exp(weights[i] - biggest)
            total += scale
            summed += scale * shares[i, step, :QH]
        out[step] = (summed / total).astype(jnp.bfloat16)


def whole(shape):
    return pl.BlockSpec(shape, lambda i, scalars: (0,) * len(shape))


def call_attention(kernel, scalars, smalls, cache, other, out_shape, name):
    own_block = (1,) + cache.shape[1:]
    return pl.pallas_call(
        kernel,
        grid_spec=pltpu.PrefetchScalarGridSpec(
            num_scalar_prefetch=1,
            grid=(1,),
            in_specs=[whole(small.shape) for small in smalls]
            + [
                pl.BlockSpec(own_block, lambda i, scalars: (scalars[0], 0, 0, 0)),
                whole(other.shape),
            ],
            out_specs=[whole(one.shape) for one in out_shape],
        ),
        out_shape=out_shape,
        compiler_params=pltpu.CompilerParams(vmem_limit_bytes=VMEM_BYTES),
        name=name,
    )(scalars, *smalls, cache, other)


def swap(value):
    return lax.ppermute(value, "core", [(0, 1), (1, 0)])


def local(q_first, kv_first, hidden_next, lengths, owners, sectioned, kv_cache):
    rep_size = lax.axis_size(REP)
    chips = lax.axis_size(CHIPS)
    core = lax.axis_index("core")
    chip = lax.axis_index(CHIPS)
    positions = kv_cache.shape[2]
    bucket_rows = sectioned.shape[1]
    width = sectioned.shape[2]

    other_cache = swap(lax.dynamic_index_in_dim(kv_cache, 1 - core, 0, keepdims=False))
    other_rows = swap(sectioned[0])

    selector = (
        owners[0][None, :] == jnp.arange(rep_size, dtype=jnp.int32)[:, None]
    ).astype(jnp.bfloat16)
    by_bucket = hidden_next.reshape(2, rep_size, bucket_rows)
    by_slot = jnp.einsum(
        "sb,rbi->rsi", selector, by_bucket, preferred_element_type=jnp.float32
    ).astype(jnp.bfloat16)
    by_slot = jnp.pad(by_slot, ((0, 0), (0, 0), (0, HD - bucket_rows)))
    hidden = lax.all_to_all(
        by_slot.reshape(2 * rep_size, 1, HD), ("core",) + REP, 0, 0, tiled=True
    ).reshape(2, rep_size, HD)[:, :, :bucket_rows]
    hidden = jnp.where(core == 0, hidden, hidden[::-1])
    partial_sum = jnp.dot(
        jnp.concatenate([hidden[0], hidden[1]], axis=1),
        jnp.concatenate([sectioned[0], other_rows], axis=0),
        preferred_element_type=jnp.float32,
    ).astype(jnp.bfloat16)

    received = lax.all_to_all(
        partial_sum.reshape(rep_size, HEADS, HD), REP, 0, 0, tiled=True
    )
    reduced = jnp.sum(received.astype(jnp.float32), axis=0)
    shares = lax.all_to_all(
        jnp.broadcast_to(reduced[None], (chips, HEADS, HD)), CHIPS, 0, 0, tiled=True
    )

    length = lax.dynamic_index_in_dim(lengths, core, 0, keepdims=False)
    shard = chip * 2 + core
    scalars = jnp.stack(
        [core, shard * positions, (chip * 2 + 1 - core) * positions, length, chip]
    ).astype(jnp.int32)
    frequency = jnp.power(
        jnp.float32(1000000.0), -(jnp.arange(HD // 2, dtype=jnp.float32) * 2.0 / HD)
    )
    angles = (length + 1).astype(jnp.float32) * frequency
    cosine = jnp.cos(angles)
    sine = jnp.sin(angles)
    cosine = jnp.concatenate([cosine, cosine])[None]
    sine = jnp.concatenate([-sine, sine])[None]
    query = lax.dynamic_index_in_dim(q_first, core, 0, keepdims=False).reshape(QH, HD)
    fresh = lax.dynamic_index_in_dim(kv_first, core, 0, keepdims=False).reshape(2 * KVH, HD)

    packed = jax.ShapeDtypeStruct((QH + 8, HD), jnp.float32)
    (first,) = call_attention(
        first_kernel, scalars, (query, fresh), kv_cache, other_cache, (packed,), "first_step"
    )
    second, made = call_attention(
        second_kernel,
        scalars,
        (shares, cosine, sine, fresh),
        kv_cache,
        other_cache,
        (packed, jax.ShapeDtypeStruct((2 * KVH, HD), jnp.bfloat16)),
        "second_step",
    )
    both = jnp.stack([first, second])
    gathered = lax.all_to_all(
        jnp.broadcast_to(both[None], (chips,) + both.shape), CHIPS, 0, 0, tiled=True
    )
    merged = pl.pallas_call(
        combine_kernel,
        out_shape=jax.ShapeDtypeStruct((2, QH, HD), jnp.bfloat16),
        name="combine",
    )(gathered)
    mine = jnp.concatenate([merged.reshape(2 * QH, HD), made], axis=0)
    theirs = swap(mine)
    pair = jnp.where(core == 0, jnp.stack([mine, theirs]), jnp.stack([theirs, mine]))
    attended = pair[:, : 2 * QH].reshape(2, 2, QH * HD)
    kv_second = pair[:, 2 * QH :].reshape(2, 2 * KVH * HD)
    return attended, kv_second


def solution(mesh):
    fine = Mesh(mesh.devices.reshape(4, 8, 2, 4, 2), ("yl", "z", "yh", "x", "core"))
    placed = (
        P(REP, None),
        P(REP, None),
        P(REP, CTX),
        P(REP),
        P(CTX, None),
        P(REP, CTX, None),
        P(REP, None, CTX, None),
    )
    return jax.shard_map(
        local,
        mesh=fine,
        in_specs=placed,
        out_specs=(P(REP, None, None), P(REP, None)),
        check_vma=False,
    )
```

time: 386 us -> 96.4 us (0.25)
  blocking collectives: 266 us -> 14 us
  waiting for transfers between devices: 75.1 us -> 23.5 us
  starting transfers between devices: 0.04 us -> 36.8 us
  between operations: 14.2 us -> 1.56 us
  matrix products: 10.6 us -> 0.48 us
  Pallas kernels: 0 us -> 5 us
  other arithmetic: 6.03 us -> 1.06 us
    all_gather x6 -> x0, blocking collectives: 170 us -> none  [joined(): pieces = jax.tree.map(lambda part: lax.all_gather(part, axis), value)]
    psum x1 -> x0, blocking collectives: 96.2 us -> none  [local(): projected = lax.psum(partial_sum, 'ctx')]
    all_gather x1 -> x0, waiting for transfers between devices: 74.4 us -> none  [local(): lax.all_gather(sectioned, 'rep', axis=0, tiled=True)]
    all_to_all x0 -> x3, waiting for transfers between devices: none -> 22.7 us  [the longest x1 9.88 us: local(): lax.all_to_all(partial_sum.reshape(rep_size, HEADS, HD), REP, 0, 0, tiled...]
    all_to_all x0 -> x3, starting transfers between devices: none -> 19.2 us  [the longest x1 8.75 us: local(): lax.all_to_all(by_slot.reshape(2 * rep_size, 1, HD), ('core',) + REP, 0,...]
    ppermute x0 -> x3, starting transfers between devices: none -> 17.6 us  [swap(): return lax.ppermute(value, 'core', [(0, 1), (1, 0)])]
    all_to_all x0 -> x1, blocking collectives: none -> 14 us  [local(): lax.all_to_all(jnp.broadcast_to(both[None], (chips,) + both.shape), CHIPS...]
    dot_general x8 -> x1, matrix products: 10.4 us -> 0.29 us  [local(): jnp.dot(jnp.concatenate([hidden[0], hidden[1]], axis=1), jnp.concatenate(...]
  transfers between devices with their start and end apart: 1 -> 6, of which waited for: 1 -> 4; matrix products, arithmetic and copies ran while one was open for 4% -> 5% of each run, Pallas kernels for 0% -> 2%
where the time goes in v1:
time: 96.4 us; the launch traced here: 94.9 us
  starting transfers between devices  36.8 us (38%)
  waiting for transfers between devices  23.5 us (24%)
  blocking collectives  14 us (15%)
  local copies, waits for them, and re-layouts  12.6 us (13%)
  Pallas kernels  5 us (5%)
  between operations  1.56 us (2%)
  other arithmetic  1.06 us (1%)
    ppermute x3, starting transfers between devices, swap(): return lax.ppermute(value, 'core', [(0, 1), (1, 0)])  17.6 us
    all_to_all x1, blocking collectives, local(): lax.all_to_all(jnp.broadcast_to(both[None], (chips,) + both.shape), CHIPS...  14 us
    all_to_all x1, waiting for transfers between devices, local(): lax.all_to_all(partial_sum.reshape(rep_size, HEADS, HD), REP, 0, 0, tiled...  9.88 us
    all_to_all x1, starting transfers between devices, local(): lax.all_to_all(by_slot.reshape(2 * rep_size, 1, HD), ('core',) + REP, 0,...  8.75 us
    all_to_all x1, waiting for transfers between devices, local(): lax.all_to_all(by_slot.reshape(2 * rep_size, 1, HD), ('core',) + REP, 0,...  7.16 us
    all_to_all x1, starting transfers between devices, local(): lax.all_to_all(jnp.broadcast_to(reduced[None], (chips, HEADS, HD)), CHIPS...  6.57 us
    unnamed x21, local copies, waits for them, and re-layouts  5.91 us
    all_to_all x1, waiting for transfers between devices, local(): lax.all_to_all(jnp.broadcast_to(reduced[None], (chips, HEADS, HD)), CHIPS...  5.63 us
  transfers between devices with their start and end apart: 6, of which 4 were waited for; matrix products, arithmetic and copies ran while one was open for 5% of the time, Pallas kernels for 2%

profile of v1, /device:TPU:1, one launch (start us, length us, event | category | flops | bytes accessed | tf_op | source)
XLA Modules:
  0.0 94.9 jit_solution(6932295703368613900)
XLA Ops:
  0.7 3.1 %dynamic-slice_bitcast_fusion = bf16[2,1024,512]{2,1,0:T(8,128)(2,1)} fusion(bf16[2,2,1024,512]{3,2,1,0:T(8,128)(2,1)} %own.3, s32[]{:T(128)S(6)} %select_n.30), kind=kLoop, calls=%fused_computation.1 | loop fusion | bytes 4194308 | tf_op jit(solution)/shard_map/jit(dynamic_index_in_dim)/squeeze | solution.py:196
  3.8 8.9 %collective-permute-start = (bf16[2,1024,512]{2,1,0:T(8,128)(2,1)}, bf16[2,1024,512]{2,1,0:T(8,128)(2,1)S(1)}, u32[]{:S(2)}, u32[]{:S(2)}) collective-permute-start(bf16[2,1024,512]{2,1,0:T(8,128)(2,1)} %dynamic-slice_bitcast_fusion), channel_id=1, source_target_pairs={{0,1},{1,0},{2,3},{3,2},{4,5},{5,4},{6,7},{7,6},{8,9},{9,8},{10,11... | collective-permute-start | bytes 6291464 | tf_op jit(solution)/shard_map/ppermute | solution.py:184
  13.1 0.6 copy.17
  13.8 8.7 %all-to-all-start = ((bf16[64,1,128]{2,1,0:T(2,128)(2,1)}), bf16[64,1,128]{2,1,0:T(2,128)(2,1)S(1)}, u32[]{:S(2)}, u32[]{:S(2)}) async-start(bf16[64,1,128]{2,1,0:T(2,128)(2,1)} %copy.17), calls=%async_computation | async-start | bytes 65536 | tf_op jit(solution)/shard_map/all_to_all | solution.py:207
  22.6 2.3 %collective-permute-start.1 = (bf16[10,5120]{1,0:T(8,128)(2,1)S(1)}, bf16[10,5120]{1,0:T(8,128)(2,1)S(1)}, u32[]{:S(2)}, u32[]{:S(2)}) collective-permute-start(bf16[10,5120]{1,0:T(8,128)(2,1)S(1)} %bitcast.47), channel_id=1, source_target_pairs={{0,1},{1,0},{2,3},{3,2},{4,5},{5,4},{6,7},{7,6},{8,9},{9,8},{10,11... | collective-permute-start | bytes 307208 | tf_op jit(solution)/shard_map/ppermute | solution.py:184
  24.8 7.2 %all-to-all-done = bf16[64,1,128]{2,1,0:T(2,128)(2,1)S(1)} async-done(((bf16[64,1,128]{2,1,0:T(2,128)(2,1)}), bf16[64,1,128]{2,1,0:T(2,128)(2,1)S(1)}, u32[]{:S(2)}, u32[]{:S(2)}) %all-to-all-start) | async-done | bytes 16416 | tf_op jit(solution)/shard_map/all_to_all | solution.py:207
  32.3 0.8 copy.21
  33.1 3.9 %all-to-all-start.1 = ((bf16[32,40,128]{2,1,0:T(8,128)(2,1)}), bf16[32,40,128]{2,1,0:T(8,128)(2,1)S(1)}, u32[]{:S(2)}, u32[]{:S(2)}) async-start(bf16[32,40,128]{2,1,0:T(8,128)(2,1)} %bitcast.24), calls=%async_computation.1 | async-start | bytes 655360 | tf_op jit(solution)/shard_map/all_to_all | solution.py:217
  37.0 0.7 dynamic_slice.16
  38.4 0.8 stack.43.scalars
  39.3 9.9 %all-to-all-done.1 = bf16[32,40,128]{2,1,0:T(8,128)(2,1)S(1)} async-done(((bf16[32,40,128]{2,1,0:T(8,128)(2,1)}), bf16[32,40,128]{2,1,0:T(8,128)(2,1)S(1)}, u32[]{:S(2)}, u32[]{:S(2)}) %all-to-all-start.1) | async-done | bytes 327712 | tf_op jit(solution)/shard_map/all_to_all | solution.py:217
  49.3 0.7 broadcast_in_dim.8
  49.9 6.6 %all-to-all-start.2 = ((f32[8,40,128]{2,1,0:T(8,128)}), f32[8,40,128]{2,1,0:T(8,128)S(1)}, u32[]{:S(2)}, u32[]{:S(2)}) async-start(f32[8,40,128]{2,1,0:T(8,128)} %broadcast_in_dim.8), calls=%async_computation.2 | async-start | bytes 327680 | tf_op jit(solution)/shard_map/all_to_all | solution.py:221
  56.7 2.2 %copy-done.1 = bf16[2,2,1024,512]{3,2,1,0:T(8,128)(2,1)S(1)} copy-done((bf16[2,2,1024,512]{3,2,1,0:T(8,128)(2,1)S(1)}, bf16[2,2,1024,512]{3,2,1,0:T(8,128)(2,1)}, u32[]{:S(2)}) %copy-start.1) | copy-done | bytes 4194328
  58.9 1.6 %first_step.1 = f32[40,128]{1,0:T(8,128)S(1)} custom-call(s32[5]{0:T(128)S(1)} %stack.43.scalars, bf16[32,128]{1,0:T(8,128)(2,1)S(1)} %bitcast.43, bf16[8,128]{1,0:T(8,128)(2,1)S(1)} %bitcast.45, bf16[2,2,1024,512]{3,2,1,0:T(8,128)(2,1)S(1)} %copy-done.1, bf16[2,1024,512]{2,1,0:T(8,128)(2,1)S(1)} %collective-permute-done.other), custom_call_target="tpu_custom_call" | custom-call | tf_op jit(solution)/shard_map/first_step/pallas_call | solution.py:165
  60.5 5.6 %all-to-all-done.2.shares = f32[8,40,128]{2,1,0:T(8,128)S(1)} async-done(((f32[8,40,128]{2,1,0:T(8,128)}), f32[8,40,128]{2,1,0:T(8,128)S(1)}, u32[]{:S(2)}, u32[]{:S(2)}) %all-to-all-start.2) | async-done | bytes 163872 | tf_op jit(solution)/shard_map/all_to_all | solution.py:221
  66.1 2.2 %copy-done.2 = bf16[2,2,1024,512]{3,2,1,0:T(8,128)(2,1)S(1)} copy-done((bf16[2,2,1024,512]{3,2,1,0:T(8,128)(2,1)S(1)}, bf16[2,2,1024,512]{3,2,1,0:T(8,128)(2,1)}, u32[]{:S(2)}) %copy-start.2) | copy-done | bytes 4194328
  68.3 1.6 %second_step.1 = (f32[40,128]{1,0:T(8,128)S(1)}, bf16[8,128]{1,0:T(8,128)(2,1)S(1)}) custom-call(s32[5]{0:T(128)S(1)} %stack.43.scalars, f32[8,40,128]{2,1,0:T(8,128)S(1)} %all-to-all-done.2.shares, f32[1,128]{1,0:T(1,128)S(1)} %maximum_bitcast_fusion.cosine, f32[1,128]{1,0:T(1,128)S(1)} %maximum_bitcast_fusion.1.sine, bf16[8,128]{1,0:T(8,128)(2,1)S(1)} %bitcast.46, ...), custom_call_target="tpu_custom_call" | custom-call | tf_op jit(solution)/shard_map/second_step/pallas_call | solution.py:165
  70.0 14.0 %all_to_all.20.shares = f32[8,2,40,128]{3,2,1,0:T(8,128)} all-to-all(f32[8,2,40,128]{3,2,1,0:T(8,128)S(1)} %broadcast_in_dim.22), channel_id=1, replica_groups=mesh['yl'=4,'z'=8,'yh'=2,'x'=4,'core'=2] {'yh','x'}, dimensions={0} | all-to-all | bytes 655360 | tf_op jit(solution)/shard_map/all_to_all | solution.py:255
  84.0 1.8 %combine.1 = bf16[2,32,128]{2,1,0:T(8,128)(2,1)} custom-call(f32[8,2,40,128]{3,2,1,0:T(8,128)} %all_to_all.20.shares), custom_call_target="tpu_custom_call" | custom-call | tf_op jit(solution)/shard_map/combine/pallas_call | solution.py:258
  85.7 0.7 fusion.15
  86.5 6.4 %collective-permute-start.2 = (bf16[72,128]{1,0:T(8,128)(2,1)S(1)}, bf16[72,128]{1,0:T(8,128)(2,1)S(1)}, u32[]{:S(2)}, u32[]{:S(2)}) collective-permute-start(bf16[72,128]{1,0:T(8,128)(2,1)S(1)} %get-tuple-element.7), channel_id=1, source_target_pairs={{0,1},{1,0},{2,3},{3,2},{4,5},{5,4},{6,7},{7,6},{8,9},{9,8},{10,11... | collective-permute-start | bytes 55304 | tf_op jit(solution)/shard_map/ppermute | solution.py:184
  92.9 0.8 collective-permute-done.2
  93.7 0.6 reshape.45
  (37 shorter events, 1.8 us)
Async XLA Ops:
  0.6 38.6 %copy-start = (bf16[2,4096]{1,0:T(2,128)(2,1)S(1)}, bf16[2,4096]{1,0:T(2,128)(2,1)}, u32[]{:S(2)}) copy-start(bf16[2,4096]{1,0:T(2,128)(2,1)} %param.7) | copy-start | bytes 49156
  0.7 12.0 %copy-start.5 = (bf16[2,320]{1,0:T(2,128)(2,1)S(1)}, bf16[2,320]{1,0:T(2,128)(2,1)}, u32[]{:S(2)}) copy-start(bf16[2,320]{1,0:T(2,128)(2,1)} %param.9) | copy-start | bytes 3844
  0.7 12.2 %copy-start.6 = (s32[1,32]{1,0:T(1,128)S(1)}, s32[1,32]{1,0:T(1,128)}, u32[]{:S(2)}) copy-start(s32[1,32]{1,0:T(1,128)} %param.11) | copy-start | bytes 388
  0.7 21.9 %copy-start.3 = (bf16[1,10,5120]{2,1,0:T(8,128)(2,1)S(1)}, bf16[1,10,5120]{2,1,0:T(8,128)(2,1)}, u32[]{:S(2)}) copy-start(bf16[1,10,5120]{2,1,0:T(8,128)(2,1)} %param.12) | copy-start | bytes 307204
  3.8 33.2 %copy-start.7 = (s32[2]{0:T(128)S(1)}, s32[2]{0:T(128)}, u32[]{:S(2)}) copy-start(s32[2]{0:T(128)} %param.10) | copy-start | bytes 28
  3.8 35.4 %copy-start.4 = (bf16[2,1024]{1,0:T(2,128)(2,1)S(1)}, bf16[2,1024]{1,0:T(2,128)(2,1)}, u32[]{:S(2)}) copy-start(bf16[2,1024]{1,0:T(2,128)(2,1)} %param.8) | copy-start | bytes 12292
  3.8 52.9 %collective-permute-start = (bf16[2,1024,512]{2,1,0:T(8,128)(2,1)}, bf16[2,1024,512]{2,1,0:T(8,128)(2,1)S(1)}, u32[]{:S(2)}, u32[]{:S(2)}) collective-permute-start(bf16[2,1024,512]{2,1,0:T(8,128)(2,1)} %dynamic-slice_bitcast_fusion), channel_id=1, source_target_pairs={{0,1},{1,0},{2,3},{3,2},{4,5},{5,4},{6,7},{7,6},{8,9},{9,8},{10,11... | collective-permute-start | bytes 6291464 | tf_op jit(solution)/shard_map/ppermute | solution.py:184
  13.8 18.2 %all-to-all-start = ((bf16[64,1,128]{2,1,0:T(2,128)(2,1)}), bf16[64,1,128]{2,1,0:T(2,128)(2,1)S(1)}, u32[]{:S(2)}, u32[]{:S(2)}) async-start(bf16[64,1,128]{2,1,0:T(2,128)(2,1)} %copy.17), calls=%async_computation | async-start | bytes 65536 | tf_op jit(solution)/shard_map/all_to_all | solution.py:207
  22.6 9.5 %collective-permute-start.1 = (bf16[10,5120]{1,0:T(8,128)(2,1)S(1)}, bf16[10,5120]{1,0:T(8,128)(2,1)S(1)}, u32[]{:S(2)}, u32[]{:S(2)}) collective-permute-start(bf16[10,5120]{1,0:T(8,128)(2,1)S(1)} %bitcast.47), channel_id=1, source_target_pairs={{0,1},{1,0},{2,3},{3,2},{4,5},{5,4},{6,7},{7,6},{8,9},{9,8},{10,11... | collective-permute-start | bytes 307208 | tf_op jit(solution)/shard_map/ppermute | solution.py:184
  33.1 16.1 %all-to-all-start.1 = ((bf16[32,40,128]{2,1,0:T(8,128)(2,1)}), bf16[32,40,128]{2,1,0:T(8,128)(2,1)S(1)}, u32[]{:S(2)}, u32[]{:S(2)}) async-start(bf16[32,40,128]{2,1,0:T(8,128)(2,1)} %bitcast.24), calls=%async_computation.1 | async-start | bytes 655360 | tf_op jit(solution)/shard_map/all_to_all | solution.py:217
  49.9 16.2 %all-to-all-start.2 = ((f32[8,40,128]{2,1,0:T(8,128)}), f32[8,40,128]{2,1,0:T(8,128)S(1)}, u32[]{:S(2)}, u32[]{:S(2)}) async-start(f32[8,40,128]{2,1,0:T(8,128)} %broadcast_in_dim.8), calls=%async_computation.2 | async-start | bytes 327680 | tf_op jit(solution)/shard_map/all_to_all | solution.py:221
  56.7 2.2 %copy-start.1 = (bf16[2,2,1024,512]{3,2,1,0:T(8,128)(2,1)S(1)}, bf16[2,2,1024,512]{3,2,1,0:T(8,128)(2,1)}, u32[]{:S(2)}) copy-start(bf16[2,2,1024,512]{3,2,1,0:T(8,128)(2,1)} %own.3) | copy-start | bytes 12582916
  66.1 2.2 %copy-start.2 = (bf16[2,2,1024,512]{3,2,1,0:T(8,128)(2,1)S(1)}, bf16[2,2,1024,512]{3,2,1,0:T(8,128)(2,1)}, u32[]{:S(2)}) copy-start(bf16[2,2,1024,512]{3,2,1,0:T(8,128)(2,1)} %own.3) | copy-start | bytes 12582916
  86.5 7.2 %collective-permute-start.2 = (bf16[72,128]{1,0:T(8,128)(2,1)S(1)}, bf16[72,128]{1,0:T(8,128)(2,1)S(1)}, u32[]{:S(2)}, u32[]{:S(2)}) collective-permute-start(bf16[72,128]{1,0:T(8,128)(2,1)S(1)} %get-tuple-element.7), channel_id=1, source_target_pairs={{0,1},{1,0},{2,3},{3,2},{4,5},{5,4},{6,7},{7,6},{8,9},{9,8},{10,11... | collective-permute-start | bytes 55304 | tf_op jit(solution)/shard_map/ppermute | solution.py:184

commit v2 on v1

v2 whole, which is shorter than its diff:
```python
import jax
import jax.numpy as jnp
import numpy as np
from jax import lax
from jax.experimental import pallas as pl
from jax.experimental.pallas import tpu as pltpu
from jax.sharding import Mesh, PartitionSpec as P

HD = 128
QH = 32
KVH = 4
PIECES = 4
GROUP = QH // KVH
HEADS = QH + 2 * KVH
REP = ("yl", "z")
CHIPS = ("yh", "x")
CTX = ("yh", "x", "core")
MASKED = -1e30
VMEM_BYTES = 16 * 1024 * 1024
BETWEEN = 1 << 35
MOST_VMEM = 48 * 1024 * 1024
ALL_VMEM = 60 * 1024 * 1024


def spread(rows):
    return jnp.concatenate(
        [jnp.broadcast_to(rows[g : g + 1], (GROUP, HD)) for g in range(KVH)], axis=0
    )


def fetch(cache, scratch, semaphores):
    core = lax.axis_index("core")
    rows = cache.shape[2] // PIECES
    copies = []
    for kind in range(2):
        for piece in range(PIECES):
            block = pl.ds(piece * rows, rows)
            copies.append(
                pltpu.make_async_copy(
                    cache.at[core, kind, block],
                    scratch.at[kind, block],
                    semaphores.at[kind * PIECES + piece],
                )
            )
    for copy in copies:
        copy.start()
    return copies[:PIECES], copies[PIECES:]


def attend(query, copies, other, scratch, length, extras):
    _, core, chip = place()
    positions = scratch.shape[1]
    halves = (
        (other, (chip * 2 + 1 - core) * positions),
        (scratch, (chip * 2 + core) * positions),
    )
    wide = query.astype(jnp.float32)
    singles = []
    for key_rows, _, counted in extras:
        score = jnp.sum(wide * spread(key_rows.astype(jnp.float32)), axis=1, keepdims=True)
        singles.append(jnp.where(counted, score * HD ** (-0.5), MASKED))
    parts = []
    for cache, start in halves:
        if cache is scratch:
            for copy in copies[0]:
                copy.wait()
        scores = jnp.concatenate(
            [
                lax.dot_general(
                    query[g * GROUP : (g + 1) * GROUP],
                    cache[0, :, g * HD : (g + 1) * HD],
                    (((1,), (1,)), ((), ())),
                    preferred_element_type=jnp.float32,
                )
                for g in range(KVH)
            ],
            axis=0,
        ) * HD ** (-0.5)
        position = start + lax.broadcasted_iota(jnp.int32, (1, positions), 1)
        parts.append(jnp.where(position < length, scores, MASKED))
    biggest = jnp.maximum(
        jnp.max(parts[0], axis=1, keepdims=True), jnp.max(parts[1], axis=1, keepdims=True)
    )
    for score in singles:
        biggest = jnp.maximum(biggest, score)
    total = jnp.zeros((QH, 1), jnp.float32)
    summed = jnp.zeros((QH, HD), jnp.float32)
    for score, (_, value_rows, _) in zip(singles, extras):
        exponential = jnp.where(score > 0.5 * MASKED, jnp.exp(score - biggest), 0.0)
        total += exponential
        rounded = exponential.astype(jnp.bfloat16).astype(jnp.float32)
        summed += rounded * spread(value_rows.astype(jnp.float32))
    for (cache, _), part in zip(halves, parts):
        exponentials = jnp.where(part > 0.5 * MASKED, jnp.exp(part - biggest), 0.0)
        total += jnp.sum(exponentials, axis=1, keepdims=True)
        rounded = exponentials.astype(jnp.bfloat16)
        if cache is scratch:
            for copy in copies[1]:
                copy.wait()
        summed += jnp.concatenate(
            [
                jnp.dot(
                    rounded[g * GROUP : (g + 1) * GROUP],
                    cache[1, :, g * HD : (g + 1) * HD],
                    preferred_element_type=jnp.float32,
                )
                for g in range(KVH)
            ],
            axis=0,
        )
    used = total > 0.0
    safe = jnp.where(used, total, 1.0)
    return summed / safe, jnp.where(used, biggest + jnp.log(safe), MASKED)


def as_row(column):
    rows = column.shape[0]
    diagonal = lax.broadcasted_iota(jnp.int32, (rows, HD), 0) == lax.broadcasted_iota(
        jnp.int32, (rows, HD), 1
    )
    return jnp.sum(jnp.where(diagonal, column, 0.0), axis=0, keepdims=True)


def pad_lanes(row):
    return jnp.concatenate([row, jnp.zeros((1, HD - row.shape[1]), row.dtype)], axis=1)


def as_column(row, rows):
    diagonal = lax.broadcasted_iota(jnp.int32, (rows, HD), 0) == lax.broadcasted_iota(
        jnp.int32, (rows, HD), 1
    )
    return jnp.sum(jnp.where(diagonal, row, 0.0), axis=1, keepdims=True)


def pack(attended, weight):
    return jnp.concatenate([attended, jnp.broadcast_to(as_row(weight), (8, HD))], axis=0)


def place(lengths=None):
    core = lax.axis_index("core")
    return None if lengths is None else lengths[core], core, lax.axis_index(CHIPS)


def stage_kernel(cache, other, scratch, arrived, left):
    core = lax.axis_index("core")
    parts = arrived.shape[0] // 2
    rows = cache.shape[2] // parts
    pieces = [(kind, pl.ds(part * rows, rows)) for kind in range(2) for part in range(parts)]
    inward = [
        pltpu.make_async_copy(cache.at[1 - core, kind, block], scratch.at[kind, block], arrived.at[i])
        for i, (kind, block) in enumerate(pieces)
    ]
    outward = [
        pltpu.make_async_copy(scratch.at[kind, block], other.at[kind, block], left.at[i])
        for i, (kind, block) in enumerate(pieces)
    ]
    for copy in inward:
        copy.start()
    for first, second in zip(inward, outward):
        first.wait()
        second.start()
    for copy in outward:
        copy.wait()


def prepare_kernel(lengths, queries, fresh, frequency, cosine, sine, query, new_rows):
    core = lax.axis_index("core")
    angles = (lengths[core] + 1).astype(jnp.float32) * frequency[...]
    lane = lax.broadcasted_iota(jnp.int32, (1, HD), 1)
    cosine[...] = jnp.cos(angles)
    sine[...] = jnp.where(lane < HD // 2, -1.0, 1.0) * jnp.sin(angles)
    wide = queries[...].astype(jnp.float32)
    wide = jnp.where(core == 0, wide[0:1], wide[1:2])
    query[...] = jnp.concatenate(
        [wide[:, i * HD : (i + 1) * HD] for i in range(QH)], axis=0
    ).astype(jnp.bfloat16)
    wide = fresh[...].astype(jnp.float32)
    wide = jnp.where(core == 0, wide[0:1], wide[1:2])
    new_rows[...] = jnp.concatenate(
        [wide[:, i * HD : (i + 1) * HD] for i in range(2 * KVH)], axis=0
    ).astype(jnp.bfloat16)


def route_kernel(hidden_source, owners_source, out, hidden, owners, semaphores):
    copies = (
        pltpu.make_async_copy(hidden_source, hidden, semaphores.at[0]),
        pltpu.make_async_copy(owners_source, owners, semaphores.at[1]),
    )
    for copy in copies:
        copy.start()
    for copy in copies:
        copy.wait()
    slots = owners.shape[1]
    columns = hidden.shape[1]
    bucket_rows = columns // slots
    column = lax.broadcasted_iota(jnp.int32, (slots, columns), 1)
    first = lax.broadcasted_iota(jnp.int32, (slots, columns), 0) * bucket_rows
    inside = (column >= first) & (column < first + bucket_rows)
    owner = jnp.sum(
        jnp.where(inside, as_column(pad_lanes(owners[...].astype(jnp.float32)), slots), 0.0),
        axis=0,
        keepdims=True,
    )
    chosen = owner == lax.broadcasted_iota(jnp.int32, (slots, columns), 0).astype(jnp.float32)
    row = lax.broadcasted_iota(jnp.int32, (columns, HD), 0)
    lane = lax.broadcasted_iota(jnp.int32, (columns, HD), 1)
    bucket = jnp.floor((row.astype(jnp.float32) + 0.5) * (1.0 / bucket_rows)).astype(jnp.int32)
    fold = row == lane + bucket * bucket_rows
    fold = jnp.where(fold, 1.0, 0.0).astype(jnp.bfloat16)
    for core in range(2):
        kept = jnp.where(chosen, hidden[core : core + 1].astype(jnp.float32), 0.0)
        folded = jnp.dot(kept.astype(jnp.bfloat16), fold, preferred_element_type=jnp.float32)
        out[core * slots : (core + 1) * slots] = jnp.broadcast_to(
            folded[:, None, :], (slots, 2, HD)
        )


def project_kernel(hidden, own_rows, other_rows, out, rows, wide):
    core = lax.axis_index("core")
    bucket_rows = own_rows.shape[0]
    slots = out.shape[0]
    rows[...] = jnp.zeros_like(rows)
    rows[0:bucket_rows] = own_rows[...]
    rows[16 : 16 + bucket_rows] = other_rows[...]
    received = hidden[:, 0, :].astype(jnp.bfloat16)
    own = jnp.where(core == 0, received[:slots], received[slots:])[:, :16]
    other = jnp.where(core == 0, received[slots:], received[:slots])[:, :16]
    both = jnp.concatenate([own, other], axis=1)
    step = 8
    for start in range(0, out.shape[1], step):
        block = jnp.dot(
            both,
            rows[:, start * HD : (start + step) * HD],
            preferred_element_type=jnp.float32,
        )
        for i in range(step):
            wide[:, start + i, :] = block[:, i * HD : (i + 1) * HD]
    out[...] = wide[...].astype(jnp.bfloat16)


def reduce_kernel(received, out):
    total = received[0].astype(jnp.float32)
    for i in range(1, received.shape[0]):
        total += received[i].astype(jnp.float32)
    for i in range(out.shape[0]):
        out[i] = total


def first_kernel(lengths, query, fresh, cache, other, out, scratch, semaphores):
    copies = fetch(cache, scratch, semaphores)
    length, _, chip = place(lengths)
    attended, weight = attend(
        query[...],
        copies,
        other,
        scratch,
        length,
        ((fresh[0:KVH], fresh[KVH:], chip == 0),),
    )
    out[...] = pack(attended, weight)


def second_kernel(
    lengths, shares, cosine, sine, fresh, first, cache, other, out, scratch, semaphores
):
    copies = fetch(cache, scratch, semaphores)
    length, _, chip = place(lengths)
    projected = shares[0]
    for i in range(1, shares.shape[0]):
        projected += shares[i]
    turned = projected[: QH + KVH]
    turned = turned * cosine[...] + pltpu.roll(turned, HD // 2, 1) * sine[...]
    query = turned[:QH].astype(jnp.bfloat16)
    second = jnp.concatenate([turned[QH:], projected[QH + KVH :]], axis=0)
    rounded = second.astype(jnp.bfloat16)
    attended, weight = attend(
        query,
        copies,
        other,
        scratch,
        length,
        (
            (fresh[0:KVH], fresh[KVH:], chip == 0),
            (rounded[0:KVH], rounded[KVH:], chip == 0),
        ),
    )
    weights = as_row(jnp.concatenate([as_column(first[QH : QH + 1], QH), weight], axis=0))
    high = weights.astype(jnp.bfloat16).astype(jnp.float32)
    middle = (weights - high).astype(jnp.bfloat16).astype(jnp.float32)
    low = weights - high - middle
    payload = jnp.concatenate(
        [first[:QH], attended, second, high, middle, low, jnp.zeros((5, HD), jnp.float32)], axis=0
    ).astype(jnp.bfloat16)
    for i in range(out.shape[0]):
        out[i] = payload


def flat(rows):
    return jnp.concatenate([rows[i : i + 1] for i in range(rows.shape[0])], axis=1)


def combine_kernel(shares, attended, made):
    count = shares.shape[0] // 2
    heads = 2 * QH
    fresh = []
    for core in range(2):
        weights = []
        for i in range(count):
            share = shares[2 * i + core]
            pieces = share[heads + 2 * KVH :].astype(jnp.float32)
            weights.append(as_column(pieces[0:1] + pieces[1:2] + pieces[2:3], heads))
        biggest = weights[0]
        for weight in weights[1:]:
            biggest = jnp.maximum(biggest, weight)
        total = jnp.zeros((heads, 1), jnp.float32)
        summed = jnp.zeros((heads, HD), jnp.float32)
        for i in range(count):
            scale = jnp.exp(weights[i] - biggest)
            total += scale
            summed += scale * shares[2 * i + core, :heads].astype(jnp.float32)
        merged = summed / total
        attended[core] = jnp.concatenate([flat(merged[:QH]), flat(merged[QH:])], axis=0).astype(
            jnp.bfloat16
        )
        fresh.append(flat(shares[core, heads : heads + 2 * KVH].astype(jnp.float32)))
    made[...] = jnp.concatenate(fresh, axis=0).astype(jnp.bfloat16)


def kernel_call(
    kernel, out_shape, name, operands, spaces="", scratch=(), limit=VMEM_BYTES, work=0
):
    kinds = {"v": pltpu.VMEM, "s": pltpu.SMEM, "h": pltpu.HBM}
    spaces = spaces or "v" * len(operands)
    moved = sum(one.size * one.dtype.itemsize for one in (*operands, *out_shape))
    return pl.pallas_call(
        kernel,
        in_specs=[pl.BlockSpec(memory_space=kinds[one]) for one in spaces],
        out_specs=[pl.BlockSpec(memory_space=pltpu.VMEM)] * len(out_shape),
        out_shape=out_shape,
        scratch_shapes=scratch,
        compiler_params=pltpu.CompilerParams(vmem_limit_bytes=limit),
        cost_estimate=pl.CostEstimate(flops=work, bytes_accessed=moved, transcendentals=0),
        name=name,
    )(*operands)


def swap(value):
    return lax.ppermute(value, "core", [(0, 1), (1, 0)])


def local(q_first, kv_first, hidden_next, lengths, owners, sectioned, kv_cache):
    rep_size = lax.axis_size(REP)
    chips = lax.axis_size(CHIPS)
    core = lax.axis_index("core")
    bf16, f32 = jnp.bfloat16, jnp.float32
    shape = jax.ShapeDtypeStruct
    _, _, positions, columns = kv_cache.shape

    (by_slot,) = kernel_call(
        route_kernel,
        (shape((2 * rep_size, 2, HD), f32),),
        "route_hidden",
        (hidden_next, owners),
        spaces="hh",
        scratch=[
            pltpu.VMEM(hidden_next.shape, bf16),
            pltpu.VMEM(owners.shape, jnp.int32),
            pltpu.SemaphoreType.DMA((2,)),
        ],
        limit=ALL_VMEM,
    )
    by_slot, sectioned, kv_cache = lax.optimization_barrier((by_slot, sectioned, kv_cache))
    hidden = lax.all_to_all(by_slot, ("core",) + REP, 0, 0, tiled=True)
    other_rows = swap(sectioned[0])
    staged = pl.pallas_call(
        stage_kernel,
        in_specs=[pl.BlockSpec(memory_space=pltpu.HBM)],
        out_specs=pl.BlockSpec(memory_space=pltpu.HBM),
        out_shape=shape(kv_cache.shape[1:], bf16),
        scratch_shapes=[
            pltpu.VMEM(kv_cache.shape[1:], bf16),
            pltpu.SemaphoreType.DMA((4,)),
            pltpu.SemaphoreType.DMA((4,)),
        ],
        compiler_params=pltpu.CompilerParams(vmem_limit_bytes=ALL_VMEM),
        cost_estimate=pl.CostEstimate(flops=0, bytes_accessed=8 * positions * columns, transcendentals=0),
        name="stage_cache",
    )(kv_cache)
    hidden, other_rows, staged = lax.optimization_barrier((hidden, other_rows, staged))
    (partial_sum,) = kernel_call(
        project_kernel,
        (shape((rep_size, HEADS, HD), bf16),),
        "project",
        (hidden, sectioned[0], other_rows),
        scratch=[
            pltpu.VMEM((32, HEADS * HD), bf16),
            pltpu.VMEM((rep_size, HEADS, HD), f32),
        ],
    )
    received = lax.all_to_all(partial_sum, REP, 0, 0, tiled=True)
    other_cache = swap(staged)

    halved = np.float32(1000000.0) ** (-(np.arange(HD // 2, dtype=np.float32) * 2.0 / HD))
    frequency = jnp.asarray(np.concatenate([halved, halved])[None], f32)
    cosine, sine, query, fresh = kernel_call(
        prepare_kernel,
        (shape((1, HD), f32), shape((1, HD), f32), shape((QH, HD), bf16), shape((2 * KVH, HD), bf16)),
        "prepare_rows",
        (lengths, q_first, kv_first, frequency),
        spaces="svvv",
        work=BETWEEN,
    )
    attention_scratch = [
        pltpu.VMEM((2, positions, columns), bf16),
        pltpu.SemaphoreType.DMA((2 * PIECES,)),
    ]
    (first,) = kernel_call(
        first_kernel,
        (shape((QH + 8, HD), f32),),
        "first_step",
        (lengths, query, fresh, kv_cache, other_cache),
        spaces="svvhv",
        scratch=attention_scratch,
        limit=MOST_VMEM,
    )
    received, first, cosine, sine = lax.optimization_barrier((received, first, cosine, sine))
    (reduced,) = kernel_call(
        reduce_kernel, (shape((chips, HEADS, HD), f32),), "sum_over_replicas", (received,)
    )
    shares = lax.all_to_all(reduced, CHIPS, 0, 0, tiled=True)
    (payload,) = kernel_call(
        second_kernel,
        (shape((2 * chips, 80, HD), bf16),),
        "second_step",
        (lengths, shares, cosine, sine, fresh, first, kv_cache, other_cache),
        spaces="svvvvvhv",
        scratch=attention_scratch,
        limit=MOST_VMEM,
    )
    gathered = lax.all_to_all(payload, CTX, 0, 0, tiled=True)
    attended, made = kernel_call(
        combine_kernel,
        (shape((2, 2, QH * HD), bf16), shape((2, 2 * KVH * HD), bf16)),
        "combine",
        (gathered,),
    )
    return attended, made


def solution(mesh):
    fine = Mesh(mesh.devices.reshape(4, 8, 2, 4, 2), ("yl", "z", "yh", "x", "core"))
    placed = (
        P(REP, None),
        P(REP, None),
        P(REP, CTX),
        P(REP),
        P(CTX, None),
        P(REP, CTX, None),
        P(REP, None, CTX, None),
    )
    return jax.shard_map(
        local,
        mesh=fine,
        in_specs=placed,
        out_specs=(P(REP, None, None), P(REP, None)),
        check_vma=False,
    )
```

time: 96.4 us -> 86.7 us (0.90)
  the two profiles are of different devices: /device:TPU:1 before, /device:TPU:8 now
where the time goes in v2:
time: 86.7 us; the launch traced here: 86.3 us
  blocking collectives  36.2 us (42%)
  starting transfers between devices  24.4 us (28%)
  Pallas kernels  12.7 us (15%)
  waiting for transfers between devices  12.1 us (14%)
    all_to_all x1, blocking collectives, local(): gathered = lax.all_to_all(payload, CTX, 0, 0, tiled=True)  18.8 us
    all_to_all x1, blocking collectives, local(): shares = lax.all_to_all(reduced, CHIPS, 0, 0, tiled=True)  17.4 us
    all_to_all x1, starting transfers between devices, local(): hidden = lax.all_to_all(by_slot, ('core',) + REP, 0, 0, tiled=True)  14.4 us
    pallas_call x7, Pallas kernels, kernel_call(): pl.pallas_call(kernel, in_specs=[pl.BlockSpec(memory_space=kinds[one]) fo...  10.3 us
    all_to_all x1, starting transfers between devices, local(): received = lax.all_to_all(partial_sum, REP, 0, 0, tiled=True)  5.77 us
    all_to_all x1, waiting for transfers between devices, local(): hidden = lax.all_to_all(by_slot, ('core',) + REP, 0, 0, tiled=True)  4.45 us
    ppermute x2, starting transfers between devices, swap(): return lax.ppermute(value, 'core', [(0, 1), (1, 0)])  4.23 us
    all_to_all x1, waiting for transfers between devices, local(): received = lax.all_to_all(partial_sum, REP, 0, 0, tiled=True)  3.98 us
  transfers between devices with their start and end apart: 4, of which 3 were waited for; matrix products, arithmetic and copies ran while one was open for 0% of the time, Pallas kernels for 7%

profile of v2, /device:TPU:8, one launch (start us, length us, event | category | flops | bytes accessed | tf_op | source)
XLA Modules:
  0.0 86.3 jit_solution(15775403144047053574)
XLA Ops:
  0.6 1.6 %route_hidden.1 = f32[64,2,128]{2,1,0:T(2,128)} custom-call(bf16[2,320]{1,0:T(2,128)(2,1)} %hidden_source.1, s32[1,32]{1,0:T(1,128)} %owners_source.1), custom_call_target="tpu_custom_call" | custom-call | bytes 66944 | tf_op jit(solution)/shard_map/route_hidden/pallas_call | solution.py:335
  2.2 14.4 %all-to-all-start = ((f32[64,2,128]{2,1,0:T(2,128)}), f32[64,2,128]{2,1,0:T(2,128)S(1)}, u32[]{:S(2)}, u32[]{:S(2)}) async-start(f32[64,2,128]{2,1,0:T(2,128)} %route_hidden.1), calls=%async_computation | async-start | bytes 131072 | tf_op jit(solution)/shard_map/all_to_all | solution.py:373
  16.6 0.0 copy-start
  16.6 0.0 copy-start.1
  16.6 0.0 copy-start.2
  16.6 0.0 copy-start.3
  16.6 0.0 copy-start.4
  16.7 2.3 %collective-permute-start = (bf16[10,5120]{1,0:T(8,128)(2,1)}, bf16[10,5120]{1,0:T(8,128)(2,1)S(1)}, u32[]{:S(2)}, u32[]{:S(2)}) collective-permute-start(bf16[10,5120]{1,0:T(8,128)(2,1)} %bitcast.1), channel_id=1, source_target_pairs={{0,1},{1,0},{2,3},{3,2},{4,5},{5,4},{6,7},{7,6},{8,9},{9,8},{10,11... | collective-permute-start | bytes 307208 | tf_op jit(solution)/shard_map/ppermute | solution.py:348
  19.0 2.4 %stage_cache.1 = bf16[2,1024,512]{2,1,0:T(8,128)(2,1)} custom-call(bf16[2,2,1024,512]{3,2,1,0:T(8,128)(2,1)} %cache.2), custom_call_target="tpu_custom_call" | custom-call | bytes 4194304 | tf_op jit(solution)/shard_map/stage_cache/pallas_call | solution.py:375
  21.4 0.0 collective-permute-done.other_rows
  21.4 4.4 %all-to-all-done.hidden = f32[64,2,128]{2,1,0:T(2,128)S(1)} async-done(((f32[64,2,128]{2,1,0:T(2,128)}), f32[64,2,128]{2,1,0:T(2,128)S(1)}, u32[]{:S(2)}, u32[]{:S(2)}) %all-to-all-start) | async-done | bytes 65568 | tf_op jit(solution)/shard_map/all_to_all | solution.py:373
  25.9 0.0 copy-done
  25.9 1.3 %project.1 = bf16[32,40,128]{2,1,0:T(8,128)(2,1)} custom-call(f32[64,2,128]{2,1,0:T(2,128)S(1)} %all-to-all-done.hidden, bf16[10,5120]{1,0:T(8,128)(2,1)S(1)} %bitcast.2, bf16[10,5120]{1,0:T(8,128)(2,1)S(1)} %collective-permute-done.other_rows), custom_call_target="tpu_custom_call" | custom-call | bytes 598016 | tf_op jit(solution)/shard_map/project/pallas_call | solution.py:335
  27.2 5.8 %all-to-all-start.1 = ((bf16[32,40,128]{2,1,0:T(8,128)(2,1)}), bf16[32,40,128]{2,1,0:T(8,128)(2,1)S(1)}, u32[]{:S(2)}, u32[]{:S(2)}) async-start(bf16[32,40,128]{2,1,0:T(8,128)(2,1)} %project.1), calls=%async_computation.1 | async-start | bytes 655360 | tf_op jit(solution)/shard_map/all_to_all | solution.py:400
  33.0 1.9 %collective-permute-start.1 = (bf16[2,1024,512]{2,1,0:T(8,128)(2,1)}, bf16[2,1024,512]{2,1,0:T(8,128)(2,1)S(1)}, u32[]{:S(2)}, u32[]{:S(2)}) collective-permute-start(bf16[2,1024,512]{2,1,0:T(8,128)(2,1)} %stage_cache.1), channel_id=1, source_target_pairs={{0,1},{1,0},{2,3},{3,2},{4,5},{5,4},{6,7},{7,6},{8,9},{9,8},{10,11... | collective-permute-start | bytes 6291464 | tf_op jit(solution)/shard_map/ppermute | solution.py:348
  35.0 0.6 prepare_rows.1
  35.6 3.7 %collective-permute-done.1.other = bf16[2,1024,512]{2,1,0:T(8,128)(2,1)S(1)} collective-permute-done((bf16[2,1024,512]{2,1,0:T(8,128)(2,1)}, bf16[2,1024,512]{2,1,0:T(8,128)(2,1)S(1)}, u32[]{:S(2)}, u32[]{:S(2)}) %collective-permute-start.1) | collective-permute-done | bytes 2097184 | tf_op jit(solution)/shard_map/ppermute | solution.py:348
  39.3 2.8 %first_step.1.first = f32[40,128]{1,0:T(8,128)S(1)} custom-call(s32[2]{0:T(128)S(1)} %copy-done.1, bf16[32,128]{1,0:T(8,128)(2,1)S(1)} %get-tuple-element.21.query, bf16[8,128]{1,0:T(8,128)(2,1)S(1)} %get-tuple-element.22.fresh, bf16[2,2,1024,512]{3,2,1,0:T(8,128)(2,1)} %cache.2, bf16[2,1024,512]{2,1,0:T(8,128)(2,1)S(1)} %collective-permute-done.1.other), custom_call_target="tpu_custom_call" | custom-call | bytes 6322184 | tf_op jit(solution)/shard_map/first_step/pallas_call | solution.py:335
  42.1 4.0 %all-to-all-done.1.received = bf16[32,40,128]{2,1,0:T(8,128)(2,1)S(1)} async-done(((bf16[32,40,128]{2,1,0:T(8,128)(2,1)}), bf16[32,40,128]{2,1,0:T(8,128)(2,1)S(1)}, u32[]{:S(2)}, u32[]{:S(2)}) %all-to-all-start.1) | async-done | bytes 327712 | tf_op jit(solution)/shard_map/all_to_all | solution.py:400
  46.1 0.1 sum_over_replicas.1
  46.2 17.4 %all_to_all.20.shares = f32[8,40,128]{2,1,0:T(8,128)S(1)} all-to-all(f32[8,40,128]{2,1,0:T(8,128)S(1)} %sum_over_replicas.1), channel_id=1, replica_groups=mesh['yl'=4,'z'=8,'yh'=2,'x'=4,'core'=2] {'yh','x'}, dimensions={0} | all-to-all | bytes 327680 | tf_op jit(solution)/shard_map/all_to_all | solution.py:430
  63.6 2.9 %second_step.1 = bf16[16,80,128]{2,1,0:T(8,128)(2,1)S(1)} custom-call(s32[2]{0:T(128)S(1)} %copy-done.1, f32[8,40,128]{2,1,0:T(8,128)S(1)} %all_to_all.20.shares, f32[1,128]{1,0:T(1,128)S(1)} %get-tuple-element.27.cosine, f32[1,128]{1,0:T(1,128)S(1)} %get-tuple-element.28.sine, bf16[8,128]{1,0:T(8,128)(2,1)S(1)} %get-tuple-element.22.fresh, ...), custom_call_target="tpu_custom_call" | custom-call | bytes 6806536 | tf_op jit(solution)/shard_map/second_step/pallas_call | solution.py:335
  66.5 18.8 %all_to_all.21.shares = bf16[16,80,128]{2,1,0:T(8,128)(2,1)S(1)} all-to-all(bf16[16,80,128]{2,1,0:T(8,128)(2,1)S(1)} %second_step.1), channel_id=1, replica_groups=mesh['yl'=4,'z'=8,'yh'=2,'x'=4,'core'=2] {'yh','x','core'}, dimensions={0} | all-to-all | bytes 655360 | tf_op jit(solution)/shard_map/all_to_all | solution.py:440
  85.3 1.0 %combine.1 = (bf16[2,2,4096]{2,1,0:T(2,128)(2,1)}, bf16[2,1024]{1,0:T(2,128)(2,1)}) custom-call(bf16[16,80,128]{2,1,0:T(8,128)(2,1)S(1)} %all_to_all.21.shares), custom_call_target="tpu_custom_call" | custom-call | bytes 364544 | tf_op jit(solution)/shard_map/combine/pallas_call | solution.py:335
  (4 shorter events, 0.0 us)
Async XLA Ops:
  2.2 23.7 %all-to-all-start = ((f32[64,2,128]{2,1,0:T(2,128)}), f32[64,2,128]{2,1,0:T(2,128)S(1)}, u32[]{:S(2)}, u32[]{:S(2)}) async-start(f32[64,2,128]{2,1,0:T(2,128)} %route_hidden.1), calls=%async_computation | async-start | bytes 131072 | tf_op jit(solution)/shard_map/all_to_all | solution.py:373
  16.6 9.3 %copy-start = (bf16[1,10,5120]{2,1,0:T(8,128)(2,1)S(1)}, bf16[1,10,5120]{2,1,0:T(8,128)(2,1)}, u32[]{:S(2)}) copy-start(bf16[1,10,5120]{2,1,0:T(8,128)(2,1)} %param.13) | copy-start | bytes 307204
  16.6 18.3 %copy-start.1 = (s32[2]{0:T(128)S(1)}, s32[2]{0:T(128)}, u32[]{:S(2)}) copy-start(s32[2]{0:T(128)} %lengths.5) | copy-start | bytes 28
  16.6 18.3 %copy-start.2 = (bf16[2,4096]{1,0:T(2,128)(2,1)S(1)}, bf16[2,4096]{1,0:T(2,128)(2,1)}, u32[]{:S(2)}) copy-start(bf16[2,4096]{1,0:T(2,128)(2,1)} %queries.1) | copy-start | bytes 49156
  16.6 18.3 %copy-start.3 = (bf16[2,1024]{1,0:T(2,128)(2,1)S(1)}, bf16[2,1024]{1,0:T(2,128)(2,1)}, u32[]{:S(2)}) copy-start(bf16[2,1024]{1,0:T(2,128)(2,1)} %fresh.1) | copy-start | bytes 12292
  16.6 18.3 %copy-start.4 = (f32[1,128]{1,0:T(1,128)S(1)}, f32[1,128]{1,0:T(1,128)}, u32[]{:S(2)}) copy-start(f32[1,128]{1,0:T(1,128)} %constant.2.clone.frequency) | copy-start | bytes 1540
  16.7 4.8 %collective-permute-start = (bf16[10,5120]{1,0:T(8,128)(2,1)}, bf16[10,5120]{1,0:T(8,128)(2,1)S(1)}, u32[]{:S(2)}, u32[]{:S(2)}) collective-permute-start(bf16[10,5120]{1,0:T(8,128)(2,1)} %bitcast.1), channel_id=1, source_target_pairs={{0,1},{1,0},{2,3},{3,2},{4,5},{5,4},{6,7},{7,6},{8,9},{9,8},{10,11... | collective-permute-start | bytes 307208 | tf_op jit(solution)/shard_map/ppermute | solution.py:348
  27.2 18.9 %all-to-all-start.1 = ((bf16[32,40,128]{2,1,0:T(8,128)(2,1)}), bf16[32,40,128]{2,1,0:T(8,128)(2,1)S(1)}, u32[]{:S(2)}, u32[]{:S(2)}) async-start(bf16[32,40,128]{2,1,0:T(8,128)(2,1)} %project.1), calls=%async_computation.1 | async-start | bytes 655360 | tf_op jit(solution)/shard_map/all_to_all | solution.py:400
  33.0 6.3 %collective-permute-start.1 = (bf16[2,1024,512]{2,1,0:T(8,128)(2,1)}, bf16[2,1024,512]{2,1,0:T(8,128)(2,1)S(1)}, u32[]{:S(2)}, u32[]{:S(2)}) collective-permute-start(bf16[2,1024,512]{2,1,0:T(8,128)(2,1)} %stage_cache.1), channel_id=1, source_target_pairs={{0,1},{1,0},{2,3},{3,2},{4,5},{5,4},{6,7},{7,6},{8,9},{9,8},{10,11... | collective-permute-start | bytes 6291464 | tf_op jit(solution)/shard_map/ppermute | solution.py:348

commit v3 on v2

--- a/solution.py
+++ b/solution.py
@@ -9,7 +9,6 @@
 HD = 128
 QH = 32
 KVH = 4
-PIECES = 4
 GROUP = QH // KVH
 HEADS = QH + 2 * KVH
 REP = ("yl", "z")
@@ -17,100 +16,64 @@
 CTX = ("yh", "x", "core")
 MASKED = -1e30
 VMEM_BYTES = 16 * 1024 * 1024
-BETWEEN = 1 << 35
+BETWEEN = 1 << 36
 MOST_VMEM = 48 * 1024 * 1024
 ALL_VMEM = 60 * 1024 * 1024
 
 
 def spread(rows):
     return jnp.concatenate(
-        [jnp.broadcast_to(rows[g : g + 1], (GROUP, HD)) for g in range(KVH)], axis=0
-    )
-
-
-def fetch(cache, scratch, semaphores):
-    core = lax.axis_index("core")
-    rows = cache.shape[2] // PIECES
-    copies = []
-    for kind in range(2):
-        for piece in range(PIECES):
-            block = pl.ds(piece * rows, rows)
-            copies.append(
-                pltpu.make_async_copy(
-                    cache.at[core, kind, block],
-                    scratch.at[kind, block],
-                    semaphores.at[kind * PIECES + piece],
-                )
+        [jnp.broadcast_to(rows[g : g + 1], (2 * GROUP, HD)) for g in range(KVH)], axis=0
+    )
+
+
+def joint(first, second):
+    pieces = []
+    for g in range(KVH):
+        pieces += [first[g * GROUP : (g + 1) * GROUP], second[g * GROUP : (g + 1) * GROUP]]
+    return jnp.concatenate(pieces, axis=0)
+
+
+def by_step(rows):
+    return jnp.concatenate(
+        [
+            rows[(2 * g + step) * GROUP : (2 * g + step + 1) * GROUP]
+            for step in range(2)
+            for g in range(KVH)
+        ],
+        axis=0,
+    )
+
+
+def scored(query, keys, start, length):
+    scores = jnp.concatenate(
+        [
+            lax.dot_general(
+                query[2 * g * GROUP : 2 * (g + 1) * GROUP],
+                keys[:, g * HD : (g + 1) * HD],
+                (((1,), (1,)), ((), ())),
+                preferred_element_type=jnp.float32,
             )
-    for copy in copies:
-        copy.start()
-    return copies[:PIECES], copies[PIECES:]
-
-
-def attend(query, copies, other, scratch, length, extras):
-    _, core, chip = place()
-    positions = scratch.shape[1]
-    halves = (
-        (other, (chip * 2 + 1 - core) * positions),
-        (scratch, (chip * 2 + core) * positions),
-    )
-    wide = query.astype(jnp.float32)
-    singles = []
-    for key_rows, _, counted in extras:
-        score = jnp.sum(wide * spread(key_rows.astype(jnp.float32)), axis=1, keepdims=True)
-        singles.append(jnp.where(counted, score * HD ** (-0.5), MASKED))
-    parts = []
-    for cache, start in halves:
-        if cache is scratch:
-            for copy in copies[0]:
-                copy.wait()
-        scores = jnp.concatenate(
-            [
-                lax.dot_general(
-                    query[g * GROUP : (g + 1) * GROUP],
-                    cache[0, :, g * HD : (g + 1) * HD],
-                    (((1,), (1,)), ((), ())),
-                    preferred_element_type=jnp.float32,
-                )
-                for g in range(KVH)
-            ],
-            axis=0,
-        ) * HD ** (-0.5)
-        position = start + lax.broadcasted_iota(jnp.int32, (1, positions), 1)
-        parts.append(jnp.where(position < length, scores, MASKED))
-    biggest = jnp.maximum(
-        jnp.max(parts[0], axis=1, keepdims=True), jnp.max(parts[1], axis=1, keepdims=True)
-    )
-    for score in singles:
-        biggest = jnp.maximum(biggest, score)
-    total = jnp.zeros((QH, 1), jnp.float32)
-    summed = jnp.zeros((QH, HD), jnp.float32)
-    for score, (_, value_rows, _) in zip(singles, extras):
-        exponential = jnp.where(score > 0.5 * MASKED, jnp.exp(score - biggest), 0.0)
-        total += exponential
-        rounded = exponential.astype(jnp.bfloat16).astype(jnp.float32)
-        summed += rounded * spread(value_rows.astype(jnp.float32))
-    for (cache, _), part in zip(halves, parts):
-        exponentials = jnp.where(part > 0.5 * MASKED, jnp.exp(part - biggest), 0.0)
-        total += jnp.sum(exponentials, axis=1, keepdims=True)
-        rounded = exponentials.astype(jnp.bfloat16)
-        if cache is scratch:
-            for copy in copies[1]:
-                copy.wait()
-        summed += jnp.concatenate(
-            [
-                jnp.dot(
-                    rounded[g * GROUP : (g + 1) * GROUP],
-                    cache[1, :, g * HD : (g + 1) * HD],
-                    preferred_element_type=jnp.float32,
-                )
-                for g in range(KVH)
-            ],
-            axis=0,
-        )
-    used = total > 0.0
-    safe = jnp.where(used, total, 1.0)
-    return summed / safe, jnp.where(used, biggest + jnp.log(safe), MASKED)
+            for g in range(KVH)
+        ],
+        axis=0,
+    ) * HD ** (-0.5)
+    position = start + lax.broadcasted_iota(jnp.int32, (1, keys.shape[0]), 1)
+    return jnp.where(position < length, scores, MASKED)
+
+
+def weighted(rounded, values):
+    return jnp.concatenate(
+        [
+            jnp.dot(
+                rounded[2 * g * GROUP : 2 * (g + 1) * GROUP],
+                values[:, g * HD : (g + 1) * HD],
+                preferred_element_type=jnp.float32,
+            )
+            for g in range(KVH)
+        ],
+        axis=0,
+    )
 
 
 def as_row(column):
@@ -130,15 +93,6 @@
         jnp.int32, (rows, HD), 1
     )
     return jnp.sum(jnp.where(diagonal, row, 0.0), axis=1, keepdims=True)
-
-
-def pack(attended, weight):
-    return jnp.concatenate([attended, jnp.broadcast_to(as_row(weight), (8, HD))], axis=0)
-
-
-def place(lengths=None):
-    core = lax.axis_index("core")
-    return None if lengths is None else lengths[core], core, lax.axis_index(CHIPS)
 
 
 def stage_kernel(cache, other, scratch, arrived, left):
@@ -163,8 +117,13 @@
         copy.wait()
 
 
-def prepare_kernel(lengths, queries, fresh, frequency, cosine, sine, query, new_rows):
+def prepare_kernel(
+    lengths, queries, fresh, frequency, cache, length, cosine, sine, query, new_rows, own_keys, semaphore
+):
     core = lax.axis_index("core")
+    copy = pltpu.make_async_copy(cache.at[core, 0], own_keys, semaphore)
+    copy.start()
+    length[...] = jnp.zeros_like(length) + lengths[core]
     angles = (lengths[core] + 1).astype(jnp.float32) * frequency[...]
     lane = lax.broadcasted_iota(jnp.int32, (1, HD), 1)
     cosine[...] = jnp.cos(angles)
@@ -179,6 +138,7 @@
     new_rows[...] = jnp.concatenate(
         [wide[:, i * HD : (i + 1) * HD] for i in range(2 * KVH)], axis=0
     ).astype(jnp.bfloat16)
+    copy.wait()
 
 
 def route_kernel(hidden_source, owners_source, out, hidden, owners, semaphores):
@@ -246,53 +206,75 @@
         out[i] = total
 
 
-def first_kernel(lengths, query, fresh, cache, other, out, scratch, semaphores):
-    copies = fetch(cache, scratch, semaphores)
-    length, _, chip = place(lengths)
-    attended, weight = attend(
-        query[...],
-        copies,
-        other,
-        scratch,
-        length,
-        ((fresh[0:KVH], fresh[KVH:], chip == 0),),
-    )
-    out[...] = pack(attended, weight)
-
-
-def second_kernel(
-    lengths, shares, cosine, sine, fresh, first, cache, other, out, scratch, semaphores
+def steps_kernel(
+    length, shares, cosine, sine, first_query, fresh, cache, other, own_keys, out, own_values,
+    held, kept, semaphore,
 ):
-    copies = fetch(cache, scratch, semaphores)
-    length, _, chip = place(lengths)
+    core = lax.axis_index("core")
+    chip = lax.axis_index(CHIPS)
+    positions = own_keys.shape[0]
+    copy = pltpu.make_async_copy(cache.at[core, 1], own_values, semaphore)
+    copy.start()
+
     projected = shares[0]
     for i in range(1, shares.shape[0]):
         projected += shares[i]
     turned = projected[: QH + KVH]
     turned = turned * cosine[...] + pltpu.roll(turned, HD // 2, 1) * sine[...]
-    query = turned[:QH].astype(jnp.bfloat16)
     second = jnp.concatenate([turned[QH:], projected[QH + KVH :]], axis=0)
-    rounded = second.astype(jnp.bfloat16)
-    attended, weight = attend(
-        query,
-        copies,
-        other,
-        scratch,
-        length,
-        (
-            (fresh[0:KVH], fresh[KVH:], chip == 0),
-            (rounded[0:KVH], rounded[KVH:], chip == 0),
-        ),
-    )
-    weights = as_row(jnp.concatenate([as_column(first[QH : QH + 1], QH), weight], axis=0))
+    query = joint(first_query[...].astype(jnp.float32), turned[:QH]).astype(jnp.bfloat16)
+    limit = length[:, 0:1]
+    parts = [
+        scored(query, other.at[0], (chip * 2 + 1 - core) * positions, limit),
+        scored(query, own_keys, (chip * 2 + core) * positions, limit),
+    ]
+
+    wide = query.astype(jnp.float32)
+    rows = 2 * QH
+    step = (lax.broadcasted_iota(jnp.int32, (rows, 1), 0) // GROUP) % 2
+    earlier = fresh[...].astype(jnp.float32)
+    later = second.astype(jnp.bfloat16).astype(jnp.float32)
+    extras = []
+    for token, counted in ((earlier, step >= 0), (later, step == 1)):
+        score = jnp.sum(wide * spread(token[:KVH]), axis=1, keepdims=True) * HD ** (-0.5)
+        extras.append(jnp.where(counted & (chip == 0), score, MASKED))
+
+    biggest = jnp.maximum(extras[0], extras[1])
+    for part in parts:
+        biggest = jnp.maximum(biggest, jnp.max(part, axis=1, keepdims=True))
+    total = jnp.zeros((rows, 1), jnp.float32)
+    summed = jnp.zeros((rows, HD), jnp.float32)
+    for score, token in zip(extras, (earlier, later)):
+        exponential = jnp.where(score > 0.5 * MASKED, jnp.exp(score - biggest), 0.0)
+        total += exponential
+        summed += exponential.astype(jnp.bfloat16).astype(jnp.float32) * spread(token[KVH:])
+    rounded = []
+    for part in parts:
+        exponentials = jnp.where(part > 0.5 * MASKED, jnp.exp(part - biggest), 0.0)
+        total += jnp.sum(exponentials, axis=1, keepdims=True)
+        rounded.append(exponentials.astype(jnp.bfloat16))
+    summed += weighted(rounded[0], other.at[1])
+    used = total > 0.0
+    safe = jnp.where(used, total, 1.0)
+    held[0] = summed
+    held[1] = jnp.broadcast_to(1.0 / safe, (rows, HD))
+    weights = as_row(by_step(jnp.where(used, biggest + jnp.log(safe), MASKED)))
     high = weights.astype(jnp.bfloat16).astype(jnp.float32)
     middle = (weights - high).astype(jnp.bfloat16).astype(jnp.float32)
     low = weights - high - middle
-    payload = jnp.concatenate(
-        [first[:QH], attended, second, high, middle, low, jnp.zeros((5, HD), jnp.float32)], axis=0
-    ).astype(jnp.bfloat16)
+    tail = jnp.concatenate([second, high, middle, low, jnp.zeros((5, HD), jnp.float32)], axis=0)
+    tail = tail.astype(jnp.bfloat16)
     for i in range(out.shape[0]):
-        out[i] = payload
+        out[i, rows:] = tail
+    kept[...] = rounded[1]
+
+    @pl.when(chip >= 0)
+    def _():
+        copy.wait()
+        attended = (held[0] + weighted(kept[...], own_values)) * held[1]
+        attended = by_step(attended).astype(jnp.bfloat16)
+        for i in range(out.shape[0]):
+            out[i, :rows] = attended
 
 
 def flat(rows):
@@ -386,7 +368,7 @@
         cost_estimate=pl.CostEstimate(flops=0, bytes_accessed=8 * positions * columns, transcendentals=0),
         name="stage_cache",
     )(kv_cache)
-    hidden, other_rows, staged = lax.optimization_barrier((hidden, other_rows, staged))
+    hidden, other_rows, _ = lax.optimization_barrier((hidden, other_rows, staged))
     (partial_sum,) = kernel_call(
         project_kernel,
         (shape((rep_size, HEADS, HD), bf16),),
@@ -397,44 +379,46 @@
             pltpu.VMEM((rep_size, HEADS, HD), f32),
         ],
     )
+    partial_sum, staged = lax.optimization_barrier((partial_sum, staged))
     received = lax.all_to_all(partial_sum, REP, 0, 0, tiled=True)
     other_cache = swap(staged)
 
     halved = np.float32(1000000.0) ** (-(np.arange(HD // 2, dtype=np.float32) * 2.0 / HD))
     frequency = jnp.asarray(np.concatenate([halved, halved])[None], f32)
-    cosine, sine, query, fresh = kernel_call(
+    length, cosine, sine, query, fresh, own_keys = kernel_call(
         prepare_kernel,
-        (shape((1, HD), f32), shape((1, HD), f32), shape((QH, HD), bf16), shape((2 * KVH, HD), bf16)),
+        (
+            shape((1, HD), jnp.int32),
+            shape((1, HD), f32),
+            shape((1, HD), f32),
+            shape((QH, HD), bf16),
+            shape((2 * KVH, HD), bf16),
+            shape((positions, columns), bf16),
+        ),
         "prepare_rows",
-        (lengths, q_first, kv_first, frequency),
-        spaces="svvv",
+        (lengths, q_first, kv_first, frequency, kv_cache),
+        spaces="svvvh",
+        scratch=[pltpu.SemaphoreType.DMA],
+        limit=52 * 1024 * 1024,
         work=BETWEEN,
     )
-    attention_scratch = [
-        pltpu.VMEM((2, positions, columns), bf16),
-        pltpu.SemaphoreType.DMA((2 * PIECES,)),
-    ]
-    (first,) = kernel_call(
-        first_kernel,
-        (shape((QH + 8, HD), f32),),
-        "first_step",
-        (lengths, query, fresh, kv_cache, other_cache),
-        spaces="svvhv",
-        scratch=attention_scratch,
-        limit=MOST_VMEM,
-    )
-    received, first, cosine, sine = lax.optimization_barrier((received, first, cosine, sine))
+    received, length = lax.optimization_barrier((received, length))
     (reduced,) = kernel_call(
         reduce_kernel, (shape((chips, HEADS, HD), f32),), "sum_over_replicas", (received,)
     )
     shares = lax.all_to_all(reduced, CHIPS, 0, 0, tiled=True)
     (payload,) = kernel_call(
-        second_kernel,
+        steps_kernel,
         (shape((2 * chips, 80, HD), bf16),),
-        "second_step",
-        (lengths, shares, cosine, sine, fresh, first, kv_cache, other_cache),
-        spaces="svvvvvhv",
-        scratch=attention_scratch,
+        "both_steps",
+        (length, shares, cosine, sine, query, fresh, kv_cache, other_cache, own_keys),
+        spaces="vvvvvvhvv",
+        scratch=[
+            pltpu.VMEM((positions, columns), bf16),
+            pltpu.VMEM((2, 2 * QH, HD), f32),
+            pltpu.VMEM((2 * QH, positions), bf16),
+            pltpu.SemaphoreType.DMA,
+        ],
         limit=MOST_VMEM,
     )
     gathered = lax.all_to_all(payload, CTX, 0, 0, tiled=True)

time: 86.7 us -> 86.2 us (level)
  Pallas kernels: 12.7 us -> 10.5 us
  waiting for transfers between devices: 12.1 us -> 13.8 us
    all_to_all x1, waiting for transfers between devices: 3.98 us -> 9.34 us  [local(): received = lax.all_to_all(partial_sum, REP, 0, 0, tiled=True)]
    ppermute x2, waiting for transfers between devices: 3.7 us -> 0.01 us  [swap(): return lax.ppermute(value, 'core', [(0, 1), (1, 0)])]
    pallas_call x7 -> x6, Pallas kernels: 10.3 us -> 8.06 us  [kernel_call(): pl.pallas_call(kernel, in_specs=[pl.BlockSpec(memory_space=kinds[one]) fo...]
  transfers between devices with their start and end apart: 4 -> 4, of which waited for: 3 -> 2; matrix products, arithmetic and copies ran while one was open for 0% -> 0% of each run, Pallas kernels for 7% -> 5%
where the time goes in v3:
time: 86.2 us; the launch traced here: 85.7 us
  blocking collectives  36.2 us (42%)
  starting transfers between devices  24.4 us (28%)
  waiting for transfers between devices  13.8 us (16%)
  Pallas kernels  10.5 us (12%)
    all_to_all x1, blocking collectives, local(): gathered = lax.all_to_all(payload, CTX, 0, 0, tiled=True)  18.8 us
    all_to_all x1, blocking collectives, local(): shares = lax.all_to_all(reduced, CHIPS, 0, 0, tiled=True)  17.4 us
    all_to_all x1, starting transfers between devices, local(): hidden = lax.all_to_all(by_slot, ('core',) + REP, 0, 0, tiled=True)  14.4 us
    all_to_all x1, waiting for transfers between devices, local(): received = lax.all_to_all(partial_sum, REP, 0, 0, tiled=True)  9.34 us
    pallas_call x6, Pallas kernels, kernel_call(): pl.pallas_call(kernel, in_specs=[pl.BlockSpec(memory_space=kinds[one]) fo...  8.06 us
    all_to_all x1, starting transfers between devices, local(): received = lax.all_to_all(partial_sum, REP, 0, 0, tiled=True)  5.77 us
    all_to_all x1, waiting for transfers between devices, local(): hidden = lax.all_to_all(by_slot, ('core',) + REP, 0, 0, tiled=True)  4.45 us
    ppermute x2, starting transfers between devices, swap(): return lax.ppermute(value, 'core', [(0, 1), (1, 0)])  4.23 us
  transfers between devices with their start and end apart: 4, of which 2 were waited for; matrix products, arithmetic and copies ran while one was open for 0% of the time, Pallas kernels for 5%

profile of v3, /device:TPU:8, one launch (start us, length us, event | category | flops | bytes accessed | tf_op | source)
XLA Modules:
  0.0 85.7 jit_solution(15572321610971056366)
XLA Ops:
  0.6 1.6 %route_hidden.1 = f32[64,2,128]{2,1,0:T(2,128)} custom-call(bf16[2,320]{1,0:T(2,128)(2,1)} %hidden_source.1, s32[1,32]{1,0:T(1,128)} %owners_source.1), custom_call_target="tpu_custom_call" | custom-call | bytes 66944 | tf_op jit(solution)/shard_map/route_hidden/pallas_call | solution.py:317
  2.2 14.4 %all-to-all-start = ((f32[64,2,128]{2,1,0:T(2,128)}), f32[64,2,128]{2,1,0:T(2,128)S(1)}, u32[]{:S(2)}, u32[]{:S(2)}) async-start(f32[64,2,128]{2,1,0:T(2,128)} %route_hidden.1), calls=%async_computation | async-start | bytes 131072 | tf_op jit(solution)/shard_map/all_to_all | solution.py:355
  16.6 0.0 copy-start
  16.6 0.0 copy-start.1
  16.6 0.0 copy-start.2
  16.6 0.0 copy-start.3
  16.6 0.0 copy-start.4
  16.7 2.3 %collective-permute-start = (bf16[10,5120]{1,0:T(8,128)(2,1)}, bf16[10,5120]{1,0:T(8,128)(2,1)S(1)}, u32[]{:S(2)}, u32[]{:S(2)}) collective-permute-start(bf16[10,5120]{1,0:T(8,128)(2,1)} %bitcast.1), channel_id=1, source_target_pairs={{0,1},{1,0},{2,3},{3,2},{4,5},{5,4},{6,7},{7,6},{8,9},{9,8},{10,11... | collective-permute-start | bytes 307208 | tf_op jit(solution)/shard_map/ppermute | solution.py:330
  19.0 2.4 %stage_cache.1 = bf16[2,1024,512]{2,1,0:T(8,128)(2,1)} custom-call(bf16[2,2,1024,512]{3,2,1,0:T(8,128)(2,1)} %cache.2), custom_call_target="tpu_custom_call" | custom-call | bytes 4194304 | tf_op jit(solution)/shard_map/stage_cache/pallas_call | solution.py:357
  21.4 0.0 collective-permute-done.other_rows
  21.4 4.4 %all-to-all-done.hidden = f32[64,2,128]{2,1,0:T(2,128)S(1)} async-done(((f32[64,2,128]{2,1,0:T(2,128)}), f32[64,2,128]{2,1,0:T(2,128)S(1)}, u32[]{:S(2)}, u32[]{:S(2)}) %all-to-all-start) | async-done | bytes 65568 | tf_op jit(solution)/shard_map/all_to_all | solution.py:355
  25.9 0.0 copy-done
  25.9 1.3 %project.1 = bf16[32,40,128]{2,1,0:T(8,128)(2,1)} custom-call(f32[64,2,128]{2,1,0:T(2,128)S(1)} %all-to-all-done.hidden, bf16[10,5120]{1,0:T(8,128)(2,1)S(1)} %bitcast.2, bf16[10,5120]{1,0:T(8,128)(2,1)S(1)} %collective-permute-done.other_rows), custom_call_target="tpu_custom_call" | custom-call | bytes 598016 | tf_op jit(solution)/shard_map/project/pallas_call | solution.py:317
  27.2 5.8 %all-to-all-start.1 = ((bf16[32,40,128]{2,1,0:T(8,128)(2,1)}), bf16[32,40,128]{2,1,0:T(8,128)(2,1)S(1)}, u32[]{:S(2)}, u32[]{:S(2)}) async-start(bf16[32,40,128]{2,1,0:T(8,128)(2,1)} %project.1), calls=%async_computation.1 | async-start | bytes 655360 | tf_op jit(solution)/shard_map/all_to_all | solution.py:383
  33.0 1.9 %collective-permute-start.1 = (bf16[2,1024,512]{2,1,0:T(8,128)(2,1)}, bf16[2,1024,512]{2,1,0:T(8,128)(2,1)S(1)}, u32[]{:S(2)}, u32[]{:S(2)}) collective-permute-start(bf16[2,1024,512]{2,1,0:T(8,128)(2,1)} %stage_cache.1), channel_id=1, source_target_pairs={{0,1},{1,0},{2,3},{3,2},{4,5},{5,4},{6,7},{7,6},{8,9},{9,8},{10,11... | collective-permute-start | bytes 6291464 | tf_op jit(solution)/shard_map/ppermute | solution.py:330
  34.9 0.0 copy-done.1
  35.0 1.8 %prepare_rows.1 = (s32[1,128]{1,0:T(1,128)S(1)}, f32[1,128]{1,0:T(1,128)S(1)}, f32[1,128]{1,0:T(1,128)S(1)}, bf16[32,128]{1,0:T(8,128)(2,1)S(1)}, bf16[8,128]{1,...) custom-call(s32[2]{0:T(128)S(1)} %copy-done.3, bf16[2,4096]{1,0:T(2,128)(2,1)S(1)} %copy-done.1, ...), custom_call_target="tpu_custom_call" | custom-call | flops 68719476736 | bytes 5275656 | tf_op jit(solution)/shard_map/prepare_rows/pallas_call | solution.py:317
  36.8 9.3 %all-to-all-done.1.received = bf16[32,40,128]{2,1,0:T(8,128)(2,1)S(1)} async-done(((bf16[32,40,128]{2,1,0:T(8,128)(2,1)}), bf16[32,40,128]{2,1,0:T(8,128)(2,1)S(1)}, u32[]{:S(2)}, u32[]{:S(2)}) %all-to-all-start.1) | async-done | bytes 327712 | tf_op jit(solution)/shard_map/all_to_all | solution.py:383
  46.1 0.1 sum_over_replicas.1
  46.2 17.4 %all_to_all.20.shares = f32[8,40,128]{2,1,0:T(8,128)S(1)} all-to-all(f32[8,40,128]{2,1,0:T(8,128)S(1)} %sum_over_replicas.1), channel_id=1, replica_groups=mesh['yl'=4,'z'=8,'yh'=2,'x'=4,'core'=2] {'yh','x'}, dimensions={0} | all-to-all | bytes 327680 | tf_op jit(solution)/shard_map/all_to_all | solution.py:409
  63.6 0.0 collective-permute-done.1.other
  63.6 2.3 %both_steps.1 = bf16[16,80,128]{2,1,0:T(8,128)(2,1)S(1)} custom-call(s32[1,128]{1,0:T(1,128)S(1)} %get-tuple-element.24.length, f32[8,40,128]{2,1,0:T(8,128)S(1)} %all_to_all.20.shares, f32[1,128]{1,0:T(1,128)S(1)} %get-tuple-element.26.cosine, f32[1,128]{1,0:T(1,128)S(1)} %get-tuple-element.27.sine, bf16[32,128]{1,0:T(8,128)(2,1)S(1)} %get-tuple-element.28.first_query, ...), custom_call_target="tpu_custom_call" | custom-call | bytes 7843328 | tf_op jit(solution)/shard_map/both_steps/pallas_call | solution.py:317
  66.0 18.8 %all_to_all.21.shares = bf16[16,80,128]{2,1,0:T(8,128)(2,1)S(1)} all-to-all(bf16[16,80,128]{2,1,0:T(8,128)(2,1)S(1)} %both_steps.1), channel_id=1, replica_groups=mesh['yl'=4,'z'=8,'yh'=2,'x'=4,'core'=2] {'yh','x','core'}, dimensions={0} | all-to-all | bytes 655360 | tf_op jit(solution)/shard_map/all_to_all | solution.py:424
  84.7 1.0 %combine.1 = (bf16[2,2,4096]{2,1,0:T(2,128)(2,1)}, bf16[2,1024]{1,0:T(2,128)(2,1)}) custom-call(bf16[16,80,128]{2,1,0:T(8,128)(2,1)S(1)} %all_to_all.21.shares), custom_call_target="tpu_custom_call" | custom-call | bytes 364544 | tf_op jit(solution)/shard_map/combine/pallas_call | solution.py:317
  (3 shorter events, 0.0 us)
Async XLA Ops:
  2.2 23.7 %all-to-all-start = ((f32[64,2,128]{2,1,0:T(2,128)}), f32[64,2,128]{2,1,0:T(2,128)S(1)}, u32[]{:S(2)}, u32[]{:S(2)}) async-start(f32[64,2,128]{2,1,0:T(2,128)} %route_hidden.1), calls=%async_computation | async-start | bytes 131072 | tf_op jit(solution)/shard_map/all_to_all | solution.py:355
  16.6 9.3 %copy-start = (bf16[1,10,5120]{2,1,0:T(8,128)(2,1)S(1)}, bf16[1,10,5120]{2,1,0:T(8,128)(2,1)}, u32[]{:S(2)}) copy-start(bf16[1,10,5120]{2,1,0:T(8,128)(2,1)} %param.13) | copy-start | bytes 307204
  16.6 18.3 %copy-start.1 = (bf16[2,4096]{1,0:T(2,128)(2,1)S(1)}, bf16[2,4096]{1,0:T(2,128)(2,1)}, u32[]{:S(2)}) copy-start(bf16[2,4096]{1,0:T(2,128)(2,1)} %queries.1) | copy-start | bytes 49156
  16.6 18.3 %copy-start.2 = (bf16[2,1024]{1,0:T(2,128)(2,1)S(1)}, bf16[2,1024]{1,0:T(2,128)(2,1)}, u32[]{:S(2)}) copy-start(bf16[2,1024]{1,0:T(2,128)(2,1)} %fresh.1) | copy-start | bytes 12292
  16.6 18.3 %copy-start.3 = (s32[2]{0:T(128)S(1)}, s32[2]{0:T(128)}, u32[]{:S(2)}) copy-start(s32[2]{0:T(128)} %lengths.1) | copy-start | bytes 28
  16.6 18.3 %copy-start.4 = (f32[1,128]{1,0:T(1,128)S(1)}, f32[1,128]{1,0:T(1,128)}, u32[]{:S(2)}) copy-start(f32[1,128]{1,0:T(1,128)} %constant.2.clone.frequency) | copy-start | bytes 1540
  16.7 4.8 %collective-permute-start = (bf16[10,5120]{1,0:T(8,128)(2,1)}, bf16[10,5120]{1,0:T(8,128)(2,1)S(1)}, u32[]{:S(2)}, u32[]{:S(2)}) collective-permute-start(bf16[10,5120]{1,0:T(8,128)(2,1)} %bitcast.1), channel_id=1, source_target_pairs={{0,1},{1,0},{2,3},{3,2},{4,5},{5,4},{6,7},{7,6},{8,9},{9,8},{10,11... | collective-permute-start | bytes 307208 | tf_op jit(solution)/shard_map/ppermute | solution.py:330
  27.2 18.9 %all-to-all-start.1 = ((bf16[32,40,128]{2,1,0:T(8,128)(2,1)}), bf16[32,40,128]{2,1,0:T(8,128)(2,1)S(1)}, u32[]{:S(2)}, u32[]{:S(2)}) async-start(bf16[32,40,128]{2,1,0:T(8,128)(2,1)} %project.1), calls=%async_computation.1 | async-start | bytes 655360 | tf_op jit(solution)/shard_map/all_to_all | solution.py:383
  33.0 30.6 %collective-permute-start.1 = (bf16[2,1024,512]{2,1,0:T(8,128)(2,1)}, bf16[2,1024,512]{2,1,0:T(8,128)(2,1)S(1)}, u32[]{:S(2)}, u32[]{:S(2)}) collective-permute-start(bf16[2,1024,512]{2,1,0:T(8,128)(2,1)} %stage_cache.1), channel_id=1, source_target_pairs={{0,1},{1,0},{2,3},{3,2},{4,5},{5,4},{6,7},{7,6},{8,9},{9,8},{10,11... | collective-permute-start | bytes 6291464 | tf_op jit(solution)/shard_map/ppermute | solution.py:330

commit v4 on v3

--- a/solution.py
+++ b/solution.py
@@ -14,7 +14,7 @@
 REP = ("yl", "z")
 CHIPS = ("yh", "x")
 CTX = ("yh", "x", "core")
-MASKED = -1e30
+MASKED = -3e38
 VMEM_BYTES = 16 * 1024 * 1024
 BETWEEN = 1 << 36
 MOST_VMEM = 48 * 1024 * 1024
@@ -141,15 +141,7 @@
     copy.wait()
 
 
-def route_kernel(hidden_source, owners_source, out, hidden, owners, semaphores):
-    copies = (
-        pltpu.make_async_copy(hidden_source, hidden, semaphores.at[0]),
-        pltpu.make_async_copy(owners_source, owners, semaphores.at[1]),
-    )
-    for copy in copies:
-        copy.start()
-    for copy in copies:
-        copy.wait()
+def route_kernel(hidden, owners, out):
     slots = owners.shape[1]
     columns = hidden.shape[1]
     bucket_rows = columns // slots
@@ -202,6 +194,7 @@
     total = received[0].astype(jnp.float32)
     for i in range(1, received.shape[0]):
         total += received[i].astype(jnp.float32)
+    total = total.astype(jnp.bfloat16)
     for i in range(out.shape[0]):
         out[i] = total
 
@@ -215,58 +208,61 @@
     positions = own_keys.shape[0]
     copy = pltpu.make_async_copy(cache.at[core, 1], own_values, semaphore)
     copy.start()
-
-    projected = shares[0]
-    for i in range(1, shares.shape[0]):
-        projected += shares[i]
-    turned = projected[: QH + KVH]
-    turned = turned * cosine[...] + pltpu.roll(turned, HD // 2, 1) * sine[...]
-    second = jnp.concatenate([turned[QH:], projected[QH + KVH :]], axis=0)
-    query = joint(first_query[...].astype(jnp.float32), turned[:QH]).astype(jnp.bfloat16)
-    limit = length[:, 0:1]
-    parts = [
-        scored(query, other.at[0], (chip * 2 + 1 - core) * positions, limit),
-        scored(query, own_keys, (chip * 2 + core) * positions, limit),
-    ]
-
-    wide = query.astype(jnp.float32)
     rows = 2 * QH
-    step = (lax.broadcasted_iota(jnp.int32, (rows, 1), 0) // GROUP) % 2
-    earlier = fresh[...].astype(jnp.float32)
-    later = second.astype(jnp.bfloat16).astype(jnp.float32)
-    extras = []
-    for token, counted in ((earlier, step >= 0), (later, step == 1)):
-        score = jnp.sum(wide * spread(token[:KVH]), axis=1, keepdims=True) * HD ** (-0.5)
-        extras.append(jnp.where(counted & (chip == 0), score, MASKED))
-
-    biggest = jnp.maximum(extras[0], extras[1])
-    for part in parts:
-        biggest = jnp.maximum(biggest, jnp.max(part, axis=1, keepdims=True))
-    total = jnp.zeros((rows, 1), jnp.float32)
-    summed = jnp.zeros((rows, HD), jnp.float32)
-    for score, token in zip(extras, (earlier, later)):
-        exponential = jnp.where(score > 0.5 * MASKED, jnp.exp(score - biggest), 0.0)
-        total += exponential
-        summed += exponential.astype(jnp.bfloat16).astype(jnp.float32) * spread(token[KVH:])
-    rounded = []
-    for part in parts:
-        exponentials = jnp.where(part > 0.5 * MASKED, jnp.exp(part - biggest), 0.0)
-        total += jnp.sum(exponentials, axis=1, keepdims=True)
-        rounded.append(exponentials.astype(jnp.bfloat16))
-    summed += weighted(rounded[0], other.at[1])
-    used = total > 0.0
-    safe = jnp.where(used, total, 1.0)
-    held[0] = summed
-    held[1] = jnp.broadcast_to(1.0 / safe, (rows, HD))
-    weights = as_row(by_step(jnp.where(used, biggest + jnp.log(safe), MASKED)))
-    high = weights.astype(jnp.bfloat16).astype(jnp.float32)
-    middle = (weights - high).astype(jnp.bfloat16).astype(jnp.float32)
-    low = weights - high - middle
-    tail = jnp.concatenate([second, high, middle, low, jnp.zeros((5, HD), jnp.float32)], axis=0)
-    tail = tail.astype(jnp.bfloat16)
-    for i in range(out.shape[0]):
-        out[i, rows:] = tail
-    kept[...] = rounded[1]
+
+    @pl.when(chip >= 0)
+    def _():
+        projected = shares[0].astype(jnp.float32)
+        for i in range(1, shares.shape[0]):
+            projected += shares[i].astype(jnp.float32)
+        turned = projected[: QH + KVH]
+        turned = turned * cosine[...] + pltpu.roll(turned, HD // 2, 1) * sine[...]
+        second = jnp.concatenate([turned[QH:], projected[QH + KVH :]], axis=0)
+        query = joint(first_query[...].astype(jnp.float32), turned[:QH]).astype(jnp.bfloat16)
+        limit = length[:, 0:1]
+        parts = [
+            scored(query, other.at[0], (chip * 2 + 1 - core) * positions, limit),
+            scored(query, own_keys, (chip * 2 + core) * positions, limit),
+        ]
+
+        wide = query.astype(jnp.float32)
+        rows = 2 * QH
+        step = (lax.broadcasted_iota(jnp.int32, (rows, 1), 0) // GROUP) % 2
+        earlier = fresh[...].astype(jnp.float32)
+        later = second.astype(jnp.bfloat16).astype(jnp.float32)
+        extras = []
+        for token, counted in ((earlier, step >= 0), (later, step == 1)):
+            score = jnp.sum(wide * spread(token[:KVH]), axis=1, keepdims=True) * HD ** (-0.5)
+            extras.append(jnp.where(counted & (chip == 0), score, MASKED))
+
+        biggest = jnp.maximum(extras[0], extras[1])
+        for part in parts:
+            biggest = jnp.maximum(biggest, jnp.max(part, axis=1, keepdims=True))
+        total = jnp.zeros((rows, 1), jnp.float32)
+        summed = jnp.zeros((rows, HD), jnp.float32)
+        for score, token in zip(extras, (earlier, later)):
+            exponential = jnp.where(score > 0.5 * MASKED, jnp.exp(score - biggest), 0.0)
+            total += exponential
+            summed += exponential.astype(jnp.bfloat16).astype(jnp.float32) * spread(token[KVH:])
+        rounded = []
+        for part in parts:
+            exponentials = jnp.where(part > 0.5 * MASKED, jnp.exp(part - biggest), 0.0)
+            total += jnp.sum(exponentials, axis=1, keepdims=True)
+            rounded.append(exponentials.astype(jnp.bfloat16))
+        summed += weighted(rounded[0], other.at[1])
+        used = total > 0.0
+        safe = jnp.where(used, total, 1.0)
+        held[0] = summed
+        held[1] = jnp.broadcast_to(1.0 / safe, (rows, HD))
+        weights = as_row(by_step(jnp.where(used, biggest + jnp.log(safe), MASKED)))
+        high = weights.astype(jnp.bfloat16).astype(jnp.float32)
+        middle = (weights - high).astype(jnp.bfloat16).astype(jnp.float32)
+        low = weights - high - middle
+        tail = jnp.concatenate([second, high, middle, low, jnp.zeros((5, HD), jnp.float32)], axis=0)
+        tail = tail.astype(jnp.bfloat16)
+        for i in range(out.shape[0]):
+            out[i, rows:] = tail
+        kept[...] = rounded[1]
 
     @pl.when(chip >= 0)
     def _():
@@ -343,12 +339,6 @@
         (shape((2 * rep_size, 2, HD), f32),),
         "route_hidden",
         (hidden_next, owners),
-        spaces="hh",
-        scratch=[
-            pltpu.VMEM(hidden_next.shape, bf16),
-            pltpu.VMEM(owners.shape, jnp.int32),
-            pltpu.SemaphoreType.DMA((2,)),
-        ],
         limit=ALL_VMEM,
     )
     by_slot, sectioned, kv_cache = lax.optimization_barrier((by_slot, sectioned, kv_cache))
@@ -404,7 +394,7 @@
     )
     received, length = lax.optimization_barrier((received, length))
     (reduced,) = kernel_call(
-        reduce_kernel, (shape((chips, HEADS, HD), f32),), "sum_over_replicas", (received,)
+        reduce_kernel, (shape((chips, HEADS, HD), bf16),), "sum_over_replicas", (received,)
     )
     shares = lax.all_to_all(reduced, CHIPS, 0, 0, tiled=True)
     (payload,) = kernel_call(

time: 86.2 us -> 85 us (0.986)
  no operation moved by 1% of the time
where the time goes in v4:
time: 85 us; the launch traced here: 84.5 us
  blocking collectives  35.8 us (42%)
  starting transfers between devices  24.4 us (29%)
  waiting for transfers between devices  13.8 us (16%)
  Pallas kernels  9.68 us (11%)
    all_to_all x1, blocking collectives, local(): gathered = lax.all_to_all(payload, CTX, 0, 0, tiled=True)  18.8 us
    all_to_all x1, blocking collectives, local(): shares = lax.all_to_all(reduced, CHIPS, 0, 0, tiled=True)  17.1 us
    all_to_all x1, starting transfers between devices, local(): hidden = lax.all_to_all(by_slot, ('core',) + REP, 0, 0, tiled=True)  14.4 us
    all_to_all x1, waiting for transfers between devices, local(): received = lax.all_to_all(partial_sum, REP, 0, 0, tiled=True)  9.34 us
    pallas_call x6, Pallas kernels, kernel_call(): pl.pallas_call(kernel, in_specs=[pl.BlockSpec(memory_space=kinds[one]) fo...  7.23 us
    all_to_all x1, starting transfers between devices, local(): received = lax.all_to_all(partial_sum, REP, 0, 0, tiled=True)  5.77 us
    all_to_all x1, waiting for transfers between devices, local(): hidden = lax.all_to_all(by_slot, ('core',) + REP, 0, 0, tiled=True)  4.45 us
    ppermute x2, starting transfers between devices, swap(): return lax.ppermute(value, 'core', [(0, 1), (1, 0)])  4.23 us
  transfers between devices with their start and end apart: 4, of which 2 were waited for; matrix products, arithmetic and copies ran while one was open for 0% of the time, Pallas kernels for 5%

profile of v4, /device:TPU:8, one launch (start us, length us, event | category | flops | bytes accessed | tf_op | source)
XLA Modules:
  0.0 84.5 jit_solution(742631508138615516)
XLA Ops:
  0.6 1.6 %route_hidden.1 = f32[64,2,128]{2,1,0:T(2,128)} custom-call(bf16[2,320]{1,0:T(2,128)(2,1)} %hidden.1, s32[1,32]{1,0:T(1,128)} %owners.1), custom_call_target="tpu_custom_call" | custom-call | bytes 66944 | tf_op jit(solution)/shard_map/route_hidden/pallas_call | solution.py:313
  2.2 14.4 %all-to-all-start = ((f32[64,2,128]{2,1,0:T(2,128)}), f32[64,2,128]{2,1,0:T(2,128)S(1)}, u32[]{:S(2)}, u32[]{:S(2)}) async-start(f32[64,2,128]{2,1,0:T(2,128)} %route_hidden.1), calls=%async_computation | async-start | bytes 131072 | tf_op jit(solution)/shard_map/all_to_all | solution.py:345
  16.6 0.0 copy-start
  16.6 0.0 copy-start.1
  16.6 0.0 copy-start.2
  16.6 0.0 copy-start.3
  16.6 0.0 copy-start.4
  16.6 2.3 %collective-permute-start = (bf16[10,5120]{1,0:T(8,128)(2,1)}, bf16[10,5120]{1,0:T(8,128)(2,1)S(1)}, u32[]{:S(2)}, u32[]{:S(2)}) collective-permute-start(bf16[10,5120]{1,0:T(8,128)(2,1)} %bitcast.1), channel_id=1, source_target_pairs={{0,1},{1,0},{2,3},{3,2},{4,5},{5,4},{6,7},{7,6},{8,9},{9,8},{10,11... | collective-permute-start | bytes 307208 | tf_op jit(solution)/shard_map/ppermute | solution.py:326
  18.9 2.4 %stage_cache.1 = bf16[2,1024,512]{2,1,0:T(8,128)(2,1)} custom-call(bf16[2,2,1024,512]{3,2,1,0:T(8,128)(2,1)} %cache.2), custom_call_target="tpu_custom_call" | custom-call | bytes 4194304 | tf_op jit(solution)/shard_map/stage_cache/pallas_call | solution.py:347
  21.4 0.0 collective-permute-done.other_rows
  21.4 4.4 %all-to-all-done.hidden = f32[64,2,128]{2,1,0:T(2,128)S(1)} async-done(((f32[64,2,128]{2,1,0:T(2,128)}), f32[64,2,128]{2,1,0:T(2,128)S(1)}, u32[]{:S(2)}, u32[]{:S(2)}) %all-to-all-start) | async-done | bytes 65568 | tf_op jit(solution)/shard_map/all_to_all | solution.py:345
  25.9 0.0 copy-done
  25.9 1.3 %project.1 = bf16[32,40,128]{2,1,0:T(8,128)(2,1)} custom-call(f32[64,2,128]{2,1,0:T(2,128)S(1)} %all-to-all-done.hidden, bf16[10,5120]{1,0:T(8,128)(2,1)S(1)} %bitcast.2, bf16[10,5120]{1,0:T(8,128)(2,1)S(1)} %collective-permute-done.other_rows), custom_call_target="tpu_custom_call" | custom-call | bytes 598016 | tf_op jit(solution)/shard_map/project/pallas_call | solution.py:313
  27.2 5.8 %all-to-all-start.1 = ((bf16[32,40,128]{2,1,0:T(8,128)(2,1)}), bf16[32,40,128]{2,1,0:T(8,128)(2,1)S(1)}, u32[]{:S(2)}, u32[]{:S(2)}) async-start(bf16[32,40,128]{2,1,0:T(8,128)(2,1)} %project.1), calls=%async_computation.1 | async-start | bytes 655360 | tf_op jit(solution)/shard_map/all_to_all | solution.py:373
  33.0 1.9 %collective-permute-start.1 = (bf16[2,1024,512]{2,1,0:T(8,128)(2,1)}, bf16[2,1024,512]{2,1,0:T(8,128)(2,1)S(1)}, u32[]{:S(2)}, u32[]{:S(2)}) collective-permute-start(bf16[2,1024,512]{2,1,0:T(8,128)(2,1)} %stage_cache.1), channel_id=1, source_target_pairs={{0,1},{1,0},{2,3},{3,2},{4,5},{5,4},{6,7},{7,6},{8,9},{9,8},{10,11... | collective-permute-start | bytes 6291464 | tf_op jit(solution)/shard_map/ppermute | solution.py:326
  34.9 0.0 copy-done.1
  34.9 1.8 %prepare_rows.1 = (s32[1,128]{1,0:T(1,128)S(1)}, f32[1,128]{1,0:T(1,128)S(1)}, f32[1,128]{1,0:T(1,128)S(1)}, bf16[32,128]{1,0:T(8,128)(2,1)S(1)}, bf16[8,128]{1,...) custom-call(s32[2]{0:T(128)S(1)} %copy-done.3, bf16[2,4096]{1,0:T(2,128)(2,1)S(1)} %copy-done.1, ...), custom_call_target="tpu_custom_call" | custom-call | flops 68719476736 | bytes 5275656 | tf_op jit(solution)/shard_map/prepare_rows/pallas_call | solution.py:313
  36.7 9.3 %all-to-all-done.1.received = bf16[32,40,128]{2,1,0:T(8,128)(2,1)S(1)} async-done(((bf16[32,40,128]{2,1,0:T(8,128)(2,1)}), bf16[32,40,128]{2,1,0:T(8,128)(2,1)S(1)}, u32[]{:S(2)}, u32[]{:S(2)}) %all-to-all-start.1) | async-done | bytes 327712 | tf_op jit(solution)/shard_map/all_to_all | solution.py:373
  46.1 0.1 sum_over_replicas.1
  46.1 17.1 %all_to_all.20.shares = bf16[8,40,128]{2,1,0:T(8,128)(2,1)S(1)} all-to-all(bf16[8,40,128]{2,1,0:T(8,128)(2,1)S(1)} %sum_over_replicas.1), channel_id=1, replica_groups=mesh['yl'=4,'z'=8,'yh'=2,'x'=4,'core'=2] {'yh','x'}, dimensions={0} | all-to-all | bytes 163840 | tf_op jit(solution)/shard_map/all_to_all | solution.py:399
  63.2 0.0 collective-permute-done.1.other
  63.2 1.5 %both_steps.1 = bf16[16,80,128]{2,1,0:T(8,128)(2,1)S(1)} custom-call(s32[1,128]{1,0:T(1,128)S(1)} %get-tuple-element.24.length, bf16[8,40,128]{2,1,0:T(8,128)(2,1)S(1)} %all_to_all.20.shares, f32[1,128]{1,0:T(1,128)S(1)} %get-tuple-element.26.cosine, f32[1,128]{1,0:T(1,128)S(1)} %get-tuple-element.27.sine, ...), custom_call_target="tpu_custom_call" | custom-call | bytes 7761408 | tf_op jit(solution)/shard_map/both_steps/pallas_call | solution.py:313
  64.7 18.8 %all_to_all.21.shares = bf16[16,80,128]{2,1,0:T(8,128)(2,1)S(1)} all-to-all(bf16[16,80,128]{2,1,0:T(8,128)(2,1)S(1)} %both_steps.1), channel_id=1, replica_groups=mesh['yl'=4,'z'=8,'yh'=2,'x'=4,'core'=2] {'yh','x','core'}, dimensions={0} | all-to-all | bytes 655360 | tf_op jit(solution)/shard_map/all_to_all | solution.py:414
  83.5 1.0 %combine.1 = (bf16[2,2,4096]{2,1,0:T(2,128)(2,1)}, bf16[2,1024]{1,0:T(2,128)(2,1)}) custom-call(bf16[16,80,128]{2,1,0:T(8,128)(2,1)S(1)} %all_to_all.21.shares), custom_call_target="tpu_custom_call" | custom-call | bytes 364544 | tf_op jit(solution)/shard_map/combine/pallas_call | solution.py:313
  (3 shorter events, 0.0 us)
Async XLA Ops:
  2.2 23.7 %all-to-all-start = ((f32[64,2,128]{2,1,0:T(2,128)}), f32[64,2,128]{2,1,0:T(2,128)S(1)}, u32[]{:S(2)}, u32[]{:S(2)}) async-start(f32[64,2,128]{2,1,0:T(2,128)} %route_hidden.1), calls=%async_computation | async-start | bytes 131072 | tf_op jit(solution)/shard_map/all_to_all | solution.py:345
  16.6 9.3 %copy-start = (bf16[1,10,5120]{2,1,0:T(8,128)(2,1)S(1)}, bf16[1,10,5120]{2,1,0:T(8,128)(2,1)}, u32[]{:S(2)}) copy-start(bf16[1,10,5120]{2,1,0:T(8,128)(2,1)} %param.13) | copy-start | bytes 307204
  16.6 18.3 %copy-start.1 = (bf16[2,4096]{1,0:T(2,128)(2,1)S(1)}, bf16[2,4096]{1,0:T(2,128)(2,1)}, u32[]{:S(2)}) copy-start(bf16[2,4096]{1,0:T(2,128)(2,1)} %queries.1) | copy-start | bytes 49156
  16.6 18.3 %copy-start.2 = (bf16[2,1024]{1,0:T(2,128)(2,1)S(1)}, bf16[2,1024]{1,0:T(2,128)(2,1)}, u32[]{:S(2)}) copy-start(bf16[2,1024]{1,0:T(2,128)(2,1)} %fresh.1) | copy-start | bytes 12292
  16.6 18.3 %copy-start.3 = (s32[2]{0:T(128)S(1)}, s32[2]{0:T(128)}, u32[]{:S(2)}) copy-start(s32[2]{0:T(128)} %lengths.1) | copy-start | bytes 28
  16.6 18.3 %copy-start.4 = (f32[1,128]{1,0:T(1,128)S(1)}, f32[1,128]{1,0:T(1,128)}, u32[]{:S(2)}) copy-start(f32[1,128]{1,0:T(1,128)} %constant.2.clone.frequency) | copy-start | bytes 1540
  16.6 4.8 %collective-permute-start = (bf16[10,5120]{1,0:T(8,128)(2,1)}, bf16[10,5120]{1,0:T(8,128)(2,1)S(1)}, u32[]{:S(2)}, u32[]{:S(2)}) collective-permute-start(bf16[10,5120]{1,0:T(8,128)(2,1)} %bitcast.1), channel_id=1, source_target_pairs={{0,1},{1,0},{2,3},{3,2},{4,5},{5,4},{6,7},{7,6},{8,9},{9,8},{10,11... | collective-permute-start | bytes 307208 | tf_op jit(solution)/shard_map/ppermute | solution.py:326
  27.2 18.9 %all-to-all-start.1 = ((bf16[32,40,128]{2,1,0:T(8,128)(2,1)}), bf16[32,40,128]{2,1,0:T(8,128)(2,1)S(1)}, u32[]{:S(2)}, u32[]{:S(2)}) async-start(bf16[32,40,128]{2,1,0:T(8,128)(2,1)} %project.1), calls=%async_computation.1 | async-start | bytes 655360 | tf_op jit(solution)/shard_map/all_to_all | solution.py:373
  33.0 30.2 %collective-permute-start.1 = (bf16[2,1024,512]{2,1,0:T(8,128)(2,1)}, bf16[2,1024,512]{2,1,0:T(8,128)(2,1)S(1)}, u32[]{:S(2)}, u32[]{:S(2)}) collective-permute-start(bf16[2,1024,512]{2,1,0:T(8,128)(2,1)} %stage_cache.1), channel_id=1, source_target_pairs={{0,1},{1,0},{2,3},{3,2},{4,5},{5,4},{6,7},{7,6},{8,9},{9,8},{10,11... | collective-permute-start | bytes 6291464 | tf_op jit(solution)/shard_map/ppermute | solution.py:326

commit v5 on v4

--- a/solution.py
+++ b/solution.py
@@ -200,8 +200,8 @@
 
 
 def steps_kernel(
-    length, shares, cosine, sine, first_query, fresh, cache, other, own_keys, out, own_values,
-    held, kept, semaphore,
+    length, shares, cosine, sine, first_query, fresh, cache, other, own_keys, out, made,
+    own_values, held, kept, semaphore,
 ):
     core = lax.axis_index("core")
     chip = lax.axis_index(CHIPS)
@@ -258,7 +258,8 @@
         high = weights.astype(jnp.bfloat16).astype(jnp.float32)
         middle = (weights - high).astype(jnp.bfloat16).astype(jnp.float32)
         low = weights - high - middle
-        tail = jnp.concatenate([second, high, middle, low, jnp.zeros((5, HD), jnp.float32)], axis=0)
+        made[...] = second.astype(jnp.bfloat16)
+        tail = jnp.concatenate([high, middle, low, jnp.zeros((5, HD), jnp.float32)], axis=0)
         tail = tail.astype(jnp.bfloat16)
         for i in range(out.shape[0]):
             out[i, rows:] = tail
@@ -277,30 +278,34 @@
     return jnp.concatenate([rows[i : i + 1] for i in range(rows.shape[0])], axis=1)
 
 
-def combine_kernel(shares, attended, made):
-    count = shares.shape[0] // 2
-    heads = 2 * QH
+def combine_kernel(shares, made, out):
+    rows = 2 * QH
+    weights = []
+    for i in range(shares.shape[0]):
+        pieces = shares[i, rows:].astype(jnp.float32)
+        weights.append(as_column(pieces[0:1] + pieces[1:2] + pieces[2:3], rows))
+    biggest = weights[0]
+    for weight in weights[1:]:
+        biggest = jnp.maximum(biggest, weight)
+    total = jnp.zeros((rows, 1), jnp.float32)
+    summed = jnp.zeros((rows, HD), jnp.float32)
+    for i, weight in enumerate(weights):
+        scale = jnp.exp(weight - biggest)
+        total += scale
+        summed += scale * shares[i, :rows].astype(jnp.float32)
+    out[:rows] = (summed / total).astype(jnp.bfloat16)
+    out[rows:] = made[...]
+
+
+def assemble_kernel(mine, theirs, attended, made):
+    core = lax.axis_index("core")
+    own, other = mine[...].astype(jnp.float32), theirs[...].astype(jnp.float32)
     fresh = []
-    for core in range(2):
-        weights = []
-        for i in range(count):
-            share = shares[2 * i + core]
-            pieces = share[heads + 2 * KVH :].astype(jnp.float32)
-            weights.append(as_column(pieces[0:1] + pieces[1:2] + pieces[2:3], heads))
-        biggest = weights[0]
-        for weight in weights[1:]:
-            biggest = jnp.maximum(biggest, weight)
-        total = jnp.zeros((heads, 1), jnp.float32)
-        summed = jnp.zeros((heads, HD), jnp.float32)
-        for i in range(count):
-            scale = jnp.exp(weights[i] - biggest)
-            total += scale
-            summed += scale * shares[2 * i + core, :heads].astype(jnp.float32)
-        merged = summed / total
-        attended[core] = jnp.concatenate([flat(merged[:QH]), flat(merged[QH:])], axis=0).astype(
-            jnp.bfloat16
-        )
-        fresh.append(flat(shares[core, heads : heads + 2 * KVH].astype(jnp.float32)))
+    for rows in (jnp.where(core == 0, own, other), jnp.where(core == 0, other, own)):
+        attended[len(fresh)] = jnp.concatenate(
+            [flat(rows[:QH]), flat(rows[QH : 2 * QH])], axis=0
+        ).astype(jnp.bfloat16)
+        fresh.append(flat(rows[2 * QH :]))
     made[...] = jnp.concatenate(fresh, axis=0).astype(jnp.bfloat16)
 
 
@@ -397,9 +402,9 @@
         reduce_kernel, (shape((chips, HEADS, HD), bf16),), "sum_over_replicas", (received,)
     )
     shares = lax.all_to_all(reduced, CHIPS, 0, 0, tiled=True)
-    (payload,) = kernel_call(
+    payload, made = kernel_call(
         steps_kernel,
-        (shape((2 * chips, 80, HD), bf16),),
+        (shape((chips, 2 * QH + 8, HD), bf16), shape((2 * KVH, HD), bf16)),
         "both_steps",
         (length, shares, cosine, sine, query, fresh, kv_cache, other_cache, own_keys),
         spaces="vvvvvvhvv",
@@ -411,12 +416,18 @@
         ],
         limit=MOST_VMEM,
     )
-    gathered = lax.all_to_all(payload, CTX, 0, 0, tiled=True)
+    gathered = lax.all_to_all(payload, CHIPS, 0, 0, tiled=True)
+    (mine,) = kernel_call(
+        combine_kernel,
+        (shape((2 * QH + 2 * KVH, HD), bf16),),
+        "combine",
+        (gathered, made),
+    )
     attended, made = kernel_call(
-        combine_kernel,
+        assemble_kernel,
         (shape((2, 2, QH * HD), bf16), shape((2, 2 * KVH * HD), bf16)),
-        "combine",
-        (gathered,),
+        "assemble",
+        (mine, swap(mine)),
     )
     return attended, made
 

time: 85 us -> 83.9 us (0.987)
  the two profiles are of different devices: /device:TPU:8 before, /device:TPU:1 now
where the time goes in v5:
time: 83.9 us; the launch traced here: 83.4 us
  starting transfers between devices  31.7 us (38%)
  blocking collectives  27.6 us (33%)
  waiting for transfers between devices  13.7 us (16%)
  Pallas kernels  9.58 us (11%)
    all_to_all x1, blocking collectives, local(): shares = lax.all_to_all(reduced, CHIPS, 0, 0, tiled=True)  15.6 us
    all_to_all x1, starting transfers between devices, local(): hidden = lax.all_to_all(by_slot, ('core',) + REP, 0, 0, tiled=True)  15.5 us
    all_to_all x1, blocking collectives, local(): gathered = lax.all_to_all(payload, CHIPS, 0, 0, tiled=True)  11.9 us
    ppermute x3, starting transfers between devices, swap(): return lax.ppermute(value, 'core', [(0, 1), (1, 0)])  11.5 us
    all_to_all x1, waiting for transfers between devices, local(): received = lax.all_to_all(partial_sum, REP, 0, 0, tiled=True)  7.93 us
    pallas_call x7, Pallas kernels, kernel_call(): pl.pallas_call(kernel, in_specs=[pl.BlockSpec(memory_space=kinds[one]) fo...  7.13 us
    all_to_all x1, waiting for transfers between devices, local(): hidden = lax.all_to_all(by_slot, ('core',) + REP, 0, 0, tiled=True)  4.94 us
    all_to_all x1, starting transfers between devices, local(): received = lax.all_to_all(partial_sum, REP, 0, 0, tiled=True)  4.71 us
  transfers between devices with their start and end apart: 5, of which 3 were waited for; matrix products, arithmetic and copies ran while one was open for 0% of the time, Pallas kernels for 5%

profile of v5, /device:TPU:1, one launch (start us, length us, event | category | flops | bytes accessed | tf_op | source)
XLA Modules:
  0.0 83.4 jit_solution(16585535331577425424)
XLA Ops:
  0.6 1.6 %route_hidden.1 = f32[64,2,128]{2,1,0:T(2,128)} custom-call(bf16[2,320]{1,0:T(2,128)(2,1)} %hidden.1, s32[1,32]{1,0:T(1,128)} %owners.1), custom_call_target="tpu_custom_call" | custom-call | bytes 66944 | tf_op jit(solution)/shard_map/route_hidden/pallas_call | solution.py:318
  2.2 15.5 %all-to-all-start = ((f32[64,2,128]{2,1,0:T(2,128)}), f32[64,2,128]{2,1,0:T(2,128)S(1)}, u32[]{:S(2)}, u32[]{:S(2)}) async-start(f32[64,2,128]{2,1,0:T(2,128)} %route_hidden.1), calls=%async_computation | async-start | bytes 131072 | tf_op jit(solution)/shard_map/all_to_all | solution.py:350
  17.7 0.0 copy-start
  17.7 0.0 copy-start.1
  17.7 0.0 copy-start.2
  17.8 0.0 copy-start.3
  17.8 0.0 copy-start.4
  17.8 2.4 %collective-permute-start = (bf16[10,5120]{1,0:T(8,128)(2,1)}, bf16[10,5120]{1,0:T(8,128)(2,1)S(1)}, u32[]{:S(2)}, u32[]{:S(2)}) collective-permute-start(bf16[10,5120]{1,0:T(8,128)(2,1)} %bitcast.1), channel_id=1, source_target_pairs={{0,1},{1,0},{2,3},{3,2},{4,5},{5,4},{6,7},{7,6},{8,9},{9,8},{10,11... | collective-permute-start | bytes 307208 | tf_op jit(solution)/shard_map/ppermute | solution.py:331
  20.2 2.4 %stage_cache.1 = bf16[2,1024,512]{2,1,0:T(8,128)(2,1)} custom-call(bf16[2,2,1024,512]{3,2,1,0:T(8,128)(2,1)} %cache.2), custom_call_target="tpu_custom_call" | custom-call | bytes 4194304 | tf_op jit(solution)/shard_map/stage_cache/pallas_call | solution.py:352
  22.6 0.0 collective-permute-done.other_rows
  22.6 4.9 %all-to-all-done.hidden = f32[64,2,128]{2,1,0:T(2,128)S(1)} async-done(((f32[64,2,128]{2,1,0:T(2,128)}), f32[64,2,128]{2,1,0:T(2,128)S(1)}, u32[]{:S(2)}, u32[]{:S(2)}) %all-to-all-start) | async-done | bytes 65568 | tf_op jit(solution)/shard_map/all_to_all | solution.py:350
  27.6 1.4 %project.1 = bf16[32,40,128]{2,1,0:T(8,128)(2,1)} custom-call(f32[64,2,128]{2,1,0:T(2,128)S(1)} %all-to-all-done.hidden, bf16[10,5120]{1,0:T(8,128)(2,1)S(1)} %bitcast.2, bf16[10,5120]{1,0:T(8,128)(2,1)S(1)} %collective-permute-done.other_rows), custom_call_target="tpu_custom_call" | custom-call | bytes 598016 | tf_op jit(solution)/shard_map/project/pallas_call | solution.py:318
  28.9 4.7 %all-to-all-start.1 = ((bf16[32,40,128]{2,1,0:T(8,128)(2,1)}), bf16[32,40,128]{2,1,0:T(8,128)(2,1)S(1)}, u32[]{:S(2)}, u32[]{:S(2)}) async-start(bf16[32,40,128]{2,1,0:T(8,128)(2,1)} %project.1), calls=%async_computation.1 | async-start | bytes 655360 | tf_op jit(solution)/shard_map/all_to_all | solution.py:378
  33.7 2.5 %collective-permute-start.1 = (bf16[2,1024,512]{2,1,0:T(8,128)(2,1)}, bf16[2,1024,512]{2,1,0:T(8,128)(2,1)S(1)}, u32[]{:S(2)}, u32[]{:S(2)}) collective-permute-start(bf16[2,1024,512]{2,1,0:T(8,128)(2,1)} %stage_cache.1), channel_id=1, source_target_pairs={{0,1},{1,0},{2,3},{3,2},{4,5},{5,4},{6,7},{7,6},{8,9},{9,8},{10,11... | collective-permute-start | bytes 6291464 | tf_op jit(solution)/shard_map/ppermute | solution.py:331
  36.2 1.8 %prepare_rows.1 = (s32[1,128]{1,0:T(1,128)S(1)}, f32[1,128]{1,0:T(1,128)S(1)}, f32[1,128]{1,0:T(1,128)S(1)}, bf16[32,128]{1,0:T(8,128)(2,1)S(1)}, bf16[8,128]{1,...) custom-call(s32[2]{0:T(128)S(1)} %copy-done.3, bf16[2,4096]{1,0:T(2,128)(2,1)S(1)} %copy-done.1, ...), custom_call_target="tpu_custom_call" | custom-call | flops 68719476736 | bytes 5275656 | tf_op jit(solution)/shard_map/prepare_rows/pallas_call | solution.py:318
  38.0 7.9 %all-to-all-done.1.received = bf16[32,40,128]{2,1,0:T(8,128)(2,1)S(1)} async-done(((bf16[32,40,128]{2,1,0:T(8,128)(2,1)}), bf16[32,40,128]{2,1,0:T(8,128)(2,1)S(1)}, u32[]{:S(2)}, u32[]{:S(2)}) %all-to-all-start.1) | async-done | bytes 327712 | tf_op jit(solution)/shard_map/all_to_all | solution.py:378
  46.0 0.1 sum_over_replicas.1
  46.0 15.6 %all_to_all.20.shares = bf16[8,40,128]{2,1,0:T(8,128)(2,1)S(1)} all-to-all(bf16[8,40,128]{2,1,0:T(8,128)(2,1)S(1)} %sum_over_replicas.1), channel_id=1, replica_groups=mesh['yl'=4,'z'=8,'yh'=2,'x'=4,'core'=2] {'yh','x'}, dimensions={0} | all-to-all | bytes 163840 | tf_op jit(solution)/shard_map/all_to_all | solution.py:404
  61.7 1.5 %both_steps.1 = (bf16[8,72,128]{2,1,0:T(8,128)(2,1)S(1)}, bf16[8,128]{1,0:T(8,128)(2,1)S(1)}) custom-call(s32[1,128]{1,0:T(1,128)S(1)} %get-tuple-element.26.length, bf16[8,40,128]{2,1,0:T(8,128)(2,1)S(1)} %all_to_all.20.shares, f32[1,128]{1,0:T(1,128)S(1)} %get-tuple-element.28.cosine, f32[1,128]{1,0:T(1,128)S(1)} %get-tuple-element.29.sine, ...), custom_call_target="tpu_custom_call" | custom-call | bytes 7583232 | tf_op jit(solution)/shard_map/both_steps/pallas_call | solution.py:318
  63.2 11.9 %all_to_all.21.shares = bf16[8,72,128]{2,1,0:T(8,128)(2,1)S(1)} all-to-all(bf16[8,72,128]{2,1,0:T(8,128)(2,1)S(1)} %get-tuple-element.34), channel_id=1, replica_groups=mesh['yl'=4,'z'=8,'yh'=2,'x'=4,'core'=2] {'yh','x'}, dimensions={0} | all-to-all | bytes 294912 | tf_op jit(solution)/shard_map/all_to_all | solution.py:419
  75.1 0.2 combine.1.mine
  75.3 6.6 %collective-permute-start.2 = (bf16[72,128]{1,0:T(8,128)(2,1)S(1)}, bf16[72,128]{1,0:T(8,128)(2,1)S(1)}, u32[]{:S(2)}, u32[]{:S(2)}) collective-permute-start(bf16[72,128]{1,0:T(8,128)(2,1)S(1)} %combine.1.mine), channel_id=1, source_target_pairs={{0,1},{1,0},{2,3},{3,2},{4,5},{5,4},{6,7},{7,6},{8,9},{9,8},{10,11... | collective-permute-start | bytes 55304 | tf_op jit(solution)/shard_map/ppermute | solution.py:331
  81.9 0.8 collective-permute-done.2.theirs
  82.7 0.7 assemble.1
  (6 shorter events, 0.0 us)
Async XLA Ops:
  2.2 25.4 %all-to-all-start = ((f32[64,2,128]{2,1,0:T(2,128)}), f32[64,2,128]{2,1,0:T(2,128)S(1)}, u32[]{:S(2)}, u32[]{:S(2)}) async-start(f32[64,2,128]{2,1,0:T(2,128)} %route_hidden.1), calls=%async_computation | async-start | bytes 131072 | tf_op jit(solution)/shard_map/all_to_all | solution.py:350
  17.7 9.9 %copy-start = (bf16[1,10,5120]{2,1,0:T(8,128)(2,1)S(1)}, bf16[1,10,5120]{2,1,0:T(8,128)(2,1)}, u32[]{:S(2)}) copy-start(bf16[1,10,5120]{2,1,0:T(8,128)(2,1)} %param.13) | copy-start | bytes 307204
  17.7 18.5 %copy-start.1 = (bf16[2,4096]{1,0:T(2,128)(2,1)S(1)}, bf16[2,4096]{1,0:T(2,128)(2,1)}, u32[]{:S(2)}) copy-start(bf16[2,4096]{1,0:T(2,128)(2,1)} %queries.1) | copy-start | bytes 49156
  17.7 18.5 %copy-start.2 = (bf16[2,1024]{1,0:T(2,128)(2,1)S(1)}, bf16[2,1024]{1,0:T(2,128)(2,1)}, u32[]{:S(2)}) copy-start(bf16[2,1024]{1,0:T(2,128)(2,1)} %fresh.1) | copy-start | bytes 12292
  17.8 18.5 %copy-start.3 = (s32[2]{0:T(128)S(1)}, s32[2]{0:T(128)}, u32[]{:S(2)}) copy-start(s32[2]{0:T(128)} %lengths.1) | copy-start | bytes 28
  17.8 18.5 %copy-start.4 = (f32[1,128]{1,0:T(1,128)S(1)}, f32[1,128]{1,0:T(1,128)}, u32[]{:S(2)}) copy-start(f32[1,128]{1,0:T(1,128)} %constant.2.clone.frequency) | copy-start | bytes 1540
  17.8 4.9 %collective-permute-start = (bf16[10,5120]{1,0:T(8,128)(2,1)}, bf16[10,5120]{1,0:T(8,128)(2,1)S(1)}, u32[]{:S(2)}, u32[]{:S(2)}) collective-permute-start(bf16[10,5120]{1,0:T(8,128)(2,1)} %bitcast.1), channel_id=1, source_target_pairs={{0,1},{1,0},{2,3},{3,2},{4,5},{5,4},{6,7},{7,6},{8,9},{9,8},{10,11... | collective-permute-start | bytes 307208 | tf_op jit(solution)/shard_map/ppermute | solution.py:331
  28.9 17.0 %all-to-all-start.1 = ((bf16[32,40,128]{2,1,0:T(8,128)(2,1)}), bf16[32,40,128]{2,1,0:T(8,128)(2,1)S(1)}, u32[]{:S(2)}, u32[]{:S(2)}) async-start(bf16[32,40,128]{2,1,0:T(8,128)(2,1)} %project.1), calls=%async_computation.1 | async-start | bytes 655360 | tf_op jit(solution)/shard_map/all_to_all | solution.py:378
  33.7 28.0 %collective-permute-start.1 = (bf16[2,1024,512]{2,1,0:T(8,128)(2,1)}, bf16[2,1024,512]{2,1,0:T(8,128)(2,1)S(1)}, u32[]{:S(2)}, u32[]{:S(2)}) collective-permute-start(bf16[2,1024,512]{2,1,0:T(8,128)(2,1)} %stage_cache.1), channel_id=1, source_target_pairs={{0,1},{1,0},{2,3},{3,2},{4,5},{5,4},{6,7},{7,6},{8,9},{9,8},{10,11... | collective-permute-start | bytes 6291464 | tf_op jit(solution)/shard_map/ppermute | solution.py:331
  75.3 7.4 %collective-permute-start.2 = (bf16[72,128]{1,0:T(8,128)(2,1)S(1)}, bf16[72,128]{1,0:T(8,128)(2,1)S(1)}, u32[]{:S(2)}, u32[]{:S(2)}) collective-permute-start(bf16[72,128]{1,0:T(8,128)(2,1)S(1)} %combine.1.mine), channel_id=1, source_target_pairs={{0,1},{1,0},{2,3},{3,2},{4,5},{5,4},{6,7},{7,6},{8,9},{9,8},{10,11... | collective-permute-start | bytes 55304 | tf_op jit(solution)/shard_map/ppermute | solution.py:331

commit v6 on v5

--- a/solution.py
+++ b/solution.py
@@ -11,7 +11,8 @@
 KVH = 4
 GROUP = QH // KVH
 HEADS = QH + 2 * KVH
-REP = ("yl", "z")
+REP = ("yp", "yq", "z")
+FOLD = ("yp", "z")
 CHIPS = ("yh", "x")
 CTX = ("yh", "x", "core")
 MASKED = -3e38
@@ -95,7 +96,7 @@
     return jnp.sum(jnp.where(diagonal, row, 0.0), axis=1, keepdims=True)
 
 
-def stage_kernel(cache, other, scratch, arrived, left):
+def fetch_kernel(cache, own_keys, other, scratch, arrived, left, semaphore):
     core = lax.axis_index("core")
     parts = arrived.shape[0] // 2
     rows = cache.shape[2] // parts
@@ -108,21 +109,19 @@
         pltpu.make_async_copy(scratch.at[kind, block], other.at[kind, block], left.at[i])
         for i, (kind, block) in enumerate(pieces)
     ]
-    for copy in inward:
+    own = pltpu.make_async_copy(cache.at[core, 0], own_keys, semaphore)
+    for copy in (*inward, own):
         copy.start()
     for first, second in zip(inward, outward):
         first.wait()
         second.start()
+    own.wait()
     for copy in outward:
         copy.wait()
 
 
-def prepare_kernel(
-    lengths, queries, fresh, frequency, cache, length, cosine, sine, query, new_rows, own_keys, semaphore
-):
-    core = lax.axis_index("core")
-    copy = pltpu.make_async_copy(cache.at[core, 0], own_keys, semaphore)
-    copy.start()
+def prepare_kernel(lengths, queries, fresh, frequency, length, cosine, sine, query, new_rows):
+    core = lax.axis_index("core")
     length[...] = jnp.zeros_like(length) + lengths[core]
     angles = (lengths[core] + 1).astype(jnp.float32) * frequency[...]
     lane = lax.broadcasted_iota(jnp.int32, (1, HD), 1)
@@ -138,7 +137,6 @@
     new_rows[...] = jnp.concatenate(
         [wide[:, i * HD : (i + 1) * HD] for i in range(2 * KVH)], axis=0
     ).astype(jnp.bfloat16)
-    copy.wait()
 
 
 def route_kernel(hidden, owners, out):
@@ -162,29 +160,44 @@
     for core in range(2):
         kept = jnp.where(chosen, hidden[core : core + 1].astype(jnp.float32), 0.0)
         folded = jnp.dot(kept.astype(jnp.bfloat16), fold, preferred_element_type=jnp.float32)
-        out[core * slots : (core + 1) * slots] = jnp.broadcast_to(
-            folded[:, None, :], (slots, 2, HD)
-        )
-
-
-def project_kernel(hidden, own_rows, other_rows, out, rows, wide):
-    core = lax.axis_index("core")
+        column_size = slots // 4
+        for outer in range(2):
+            first = (2 * core + outer) * column_size
+            for pair in range(2):
+                block = (2 * outer + pair) * column_size
+                out[first : first + column_size, pair, :] = folded[block : block + column_size]
+
+
+def pack_kernel(own_rows, pair_rows, near_rows):
     bucket_rows = own_rows.shape[0]
+    near_rows[...] = jnp.zeros_like(near_rows)
+    near_rows[0:bucket_rows] = own_rows[...]
+    near_rows[16 : 16 + bucket_rows] = pair_rows[...]
+
+
+def project_kernel(hidden, near_rows, far_rows, far_pair, out, rows, wide):
+    core = lax.axis_index("core")
+    side = lax.axis_index("yq")
+    bucket_rows = far_rows.shape[0]
     slots = out.shape[0]
     rows[...] = jnp.zeros_like(rows)
-    rows[0:bucket_rows] = own_rows[...]
-    rows[16 : 16 + bucket_rows] = other_rows[...]
-    received = hidden[:, 0, :].astype(jnp.bfloat16)
-    own = jnp.where(core == 0, received[:slots], received[slots:])[:, :16]
-    other = jnp.where(core == 0, received[slots:], received[:slots])[:, :16]
-    both = jnp.concatenate([own, other], axis=1)
+    rows[0:bucket_rows] = far_rows[...]
+    rows[16 : 16 + bucket_rows] = far_pair[...]
+    left, right = hidden[:, 0, :], hidden[:, 1, :]
+    same = jnp.where(side == 0, left, right).astype(jnp.bfloat16)
+    next_to = jnp.where(side == 0, right, left).astype(jnp.bfloat16)
+    pieces = []
+    for mine in (True, False):
+        for one in (same, next_to):
+            first, last = one[:slots], one[slots:]
+            chosen = jnp.where((core == 0) == mine, first, last)
+            pieces.append(chosen[:, :16])
+    near, far = (jnp.concatenate(two, axis=1) for two in (pieces[:2], pieces[2:]))
     step = 8
     for start in range(0, out.shape[1], step):
-        block = jnp.dot(
-            both,
-            rows[:, start * HD : (start + step) * HD],
-            preferred_element_type=jnp.float32,
-        )
+        columns = slice(start * HD, (start + step) * HD)
+        block = jnp.dot(near, near_rows[:, columns], preferred_element_type=jnp.float32)
+        block += jnp.dot(far, rows[:, columns], preferred_element_type=jnp.float32)
         for i in range(step):
             wide[:, start + i, :] = block[:, i * HD : (i + 1) * HD]
     out[...] = wide[...].astype(jnp.bfloat16)
@@ -333,6 +346,7 @@
 
 def local(q_first, kv_first, hidden_next, lengths, owners, sectioned, kv_cache):
     rep_size = lax.axis_size(REP)
+    folded = lax.axis_size(FOLD)
     chips = lax.axis_size(CHIPS)
     core = lax.axis_index("core")
     bf16, f32 = jnp.bfloat16, jnp.float32
@@ -341,46 +355,57 @@
 
     (by_slot,) = kernel_call(
         route_kernel,
-        (shape((2 * rep_size, 2, HD), f32),),
+        (shape((rep_size, 4, HD), f32),),
         "route_hidden",
         (hidden_next, owners),
         limit=ALL_VMEM,
     )
     by_slot, sectioned, kv_cache = lax.optimization_barrier((by_slot, sectioned, kv_cache))
-    hidden = lax.all_to_all(by_slot, ("core",) + REP, 0, 0, tiled=True)
-    other_rows = swap(sectioned[0])
-    staged = pl.pallas_call(
-        stage_kernel,
+    hidden = lax.all_to_all(by_slot, ("core",) + FOLD, 0, 0, tiled=True)
+    pair_rows = lax.ppermute(sectioned[0], "yq", [(0, 1), (1, 0)])
+    far_rows = swap(sectioned[0])
+    far_pair = swap(pair_rows)
+    (near_rows,) = kernel_call(
+        pack_kernel,
+        (shape((32, HEADS * HD), bf16),),
+        "pack_rows",
+        (sectioned[0], pair_rows),
+    )
+    hidden, near_rows, far_rows, far_pair = lax.optimization_barrier(
+        (hidden, near_rows, far_rows, far_pair)
+    )
+    (partial_sum,) = kernel_call(
+        project_kernel,
+        (shape((folded, HEADS, HD), bf16),),
+        "project",
+        (hidden, near_rows, far_rows, far_pair),
+        scratch=[
+            pltpu.VMEM((32, HEADS * HD), bf16),
+            pltpu.VMEM((folded, HEADS, HD), f32),
+        ],
+    )
+    partial_sum, kv_cache = lax.optimization_barrier((partial_sum, kv_cache))
+    received = lax.all_to_all(partial_sum, FOLD, 0, 0, tiled=True)
+
+    own_keys, staged = pl.pallas_call(
+        fetch_kernel,
         in_specs=[pl.BlockSpec(memory_space=pltpu.HBM)],
-        out_specs=pl.BlockSpec(memory_space=pltpu.HBM),
-        out_shape=shape(kv_cache.shape[1:], bf16),
+        out_specs=[pl.BlockSpec(memory_space=pltpu.VMEM), pl.BlockSpec(memory_space=pltpu.HBM)],
+        out_shape=(shape((positions, columns), bf16), shape(kv_cache.shape[1:], bf16)),
         scratch_shapes=[
             pltpu.VMEM(kv_cache.shape[1:], bf16),
             pltpu.SemaphoreType.DMA((4,)),
             pltpu.SemaphoreType.DMA((4,)),
-        ],
-        compiler_params=pltpu.CompilerParams(vmem_limit_bytes=ALL_VMEM),
-        cost_estimate=pl.CostEstimate(flops=0, bytes_accessed=8 * positions * columns, transcendentals=0),
-        name="stage_cache",
+            pltpu.SemaphoreType.DMA,
+        ],
+        compiler_params=pltpu.CompilerParams(vmem_limit_bytes=52 * 1024 * 1024),
+        name="fetch_cache",
     )(kv_cache)
-    hidden, other_rows, _ = lax.optimization_barrier((hidden, other_rows, staged))
-    (partial_sum,) = kernel_call(
-        project_kernel,
-        (shape((rep_size, HEADS, HD), bf16),),
-        "project",
-        (hidden, sectioned[0], other_rows),
-        scratch=[
-            pltpu.VMEM((32, HEADS * HD), bf16),
-            pltpu.VMEM((rep_size, HEADS, HD), f32),
-        ],
-    )
-    partial_sum, staged = lax.optimization_barrier((partial_sum, staged))
-    received = lax.all_to_all(partial_sum, REP, 0, 0, tiled=True)
     other_cache = swap(staged)
-
+    lengths, own_keys = lax.optimization_barrier((lengths, own_keys))
     halved = np.float32(1000000.0) ** (-(np.arange(HD // 2, dtype=np.float32) * 2.0 / HD))
     frequency = jnp.asarray(np.concatenate([halved, halved])[None], f32)
-    length, cosine, sine, query, fresh, own_keys = kernel_call(
+    length, cosine, sine, query, fresh = kernel_call(
         prepare_kernel,
         (
             shape((1, HD), jnp.int32),
@@ -388,18 +413,18 @@
             shape((1, HD), f32),
             shape((QH, HD), bf16),
             shape((2 * KVH, HD), bf16),
-            shape((positions, columns), bf16),
         ),
         "prepare_rows",
-        (lengths, q_first, kv_first, frequency, kv_cache),
-        spaces="svvvh",
-        scratch=[pltpu.SemaphoreType.DMA],
-        limit=52 * 1024 * 1024,
-        work=BETWEEN,
+        (lengths, q_first, kv_first, frequency),
+        spaces="svvv",
     )
     received, length = lax.optimization_barrier((received, length))
     (reduced,) = kernel_call(
-        reduce_kernel, (shape((chips, HEADS, HD), bf16),), "sum_over_replicas", (received,)
+        reduce_kernel,
+        (shape((chips, HEADS, HD), bf16),),
+        "sum_over_replicas",
+        (received,),
+        work=BETWEEN,
     )
     shares = lax.all_to_all(reduced, CHIPS, 0, 0, tiled=True)
     payload, made = kernel_call(
@@ -433,7 +458,7 @@
 
 
 def solution(mesh):
-    fine = Mesh(mesh.devices.reshape(4, 8, 2, 4, 2), ("yl", "z", "yh", "x", "core"))
+    fine = Mesh(mesh.devices.reshape(2, 2, 8, 2, 4, 2), ("yp", "yq", "z", "yh", "x", "core"))
     placed = (
         P(REP, None),
         P(REP, None),

time: 83.9 us -> 82.2 us (0.980)
  starting transfers between devices: 31.7 us -> 36.7 us
  waiting for transfers between devices: 13.7 us -> 9.52 us
  blocking collectives: 27.6 us -> 25.6 us
  Pallas kernels: 9.58 us -> 8.17 us
  local copies, waits for them, and re-layouts: 0.03 us -> 0.94 us
    all_to_all x2, waiting for transfers between devices: 12.9 us -> 8.69 us  [the longest x1 4.76 us: local(): received = lax.all_to_all(partial_sum, FOLD, 0, 0, tiled=True)]
    ppermute x0 -> x1, starting transfers between devices: none -> 4.02 us  [local(): pair_rows = lax.ppermute(sectioned[0], 'yq', [(0, 1), (1, 0)])]
    ppermute x3 -> x4, starting transfers between devices: 11.5 us -> 14.4 us  [swap(): return lax.ppermute(value, 'core', [(0, 1), (1, 0)])]
    all_to_all x2, starting transfers between devices: 20.2 us -> 18.3 us  [the longest x1 13.5 us: local(): hidden = lax.all_to_all(by_slot, ('core',) + FOLD, 0, 0, tiled=True)]
    all_to_all x1, blocking collectives: 15.6 us -> 13.7 us  [local(): shares = lax.all_to_all(reduced, CHIPS, 0, 0, tiled=True)]
    pallas_call x7 -> x8, Pallas kernels: 7.13 us -> 5.7 us  [kernel_call(): pl.pallas_call(kernel, in_specs=[pl.BlockSpec(memory_space=kinds[one]) fo...]
    unnamed x10, local copies, waits for them, and re-layouts: 0.03 us -> 0.94 us
  transfers between devices with their start and end apart: 5 -> 7, of which waited for: 3 -> 3; matrix products, arithmetic and copies ran while one was open for 0% -> 0% of each run, Pallas kernels for 5% -> 4%
where the time goes in v6:
time: 82.2 us; the launch traced here: 81.7 us
  starting transfers between devices  36.7 us (45%)
  blocking collectives  25.6 us (31%)
  waiting for transfers between devices  9.52 us (12%)
  Pallas kernels  8.17 us (10%)
  local copies, waits for them, and re-layouts  0.94 us (1%)
    ppermute x4, starting transfers between devices, swap(): return lax.ppermute(value, 'core', [(0, 1), (1, 0)])  14.4 us
    all_to_all x1, blocking collectives, local(): shares = lax.all_to_all(reduced, CHIPS, 0, 0, tiled=True)  13.7 us
    all_to_all x1, starting transfers between devices, local(): hidden = lax.all_to_all(by_slot, ('core',) + FOLD, 0, 0, tiled=True)  13.5 us
    all_to_all x1, blocking collectives, local(): gathered = lax.all_to_all(payload, CHIPS, 0, 0, tiled=True)  11.9 us
    pallas_call x8, Pallas kernels, kernel_call(): pl.pallas_call(kernel, in_specs=[pl.BlockSpec(memory_space=kinds[one]) fo...  5.7 us
    all_to_all x1, starting transfers between devices, local(): received = lax.all_to_all(partial_sum, FOLD, 0, 0, tiled=True)  4.79 us
    all_to_all x1, waiting for transfers between devices, local(): received = lax.all_to_all(partial_sum, FOLD, 0, 0, tiled=True)  4.76 us
    ppermute x1, starting transfers between devices, local(): pair_rows = lax.ppermute(sectioned[0], 'yq', [(0, 1), (1, 0)])  4.02 us
  transfers between devices with their start and end apart: 7, of which 3 were waited for; matrix products, arithmetic and copies ran while one was open for 0% of the time, Pallas kernels for 4%

profile of v6, /device:TPU:1, one launch (start us, length us, event | category | flops | bytes accessed | tf_op | source)
XLA Modules:
  0.0 81.7 jit_solution(4472342770233040485)
XLA Ops:
  0.6 1.6 %route_hidden.1 = f32[32,4,128]{2,1,0:T(4,128)} custom-call(bf16[2,320]{1,0:T(2,128)(2,1)} %hidden.1, s32[1,32]{1,0:T(1,128)} %owners.1), custom_call_target="tpu_custom_call" | custom-call | bytes 66944 | tf_op jit(solution)/shard_map/route_hidden/pallas_call | solution.py:331
  2.2 4.0 %collective-permute-start = (bf16[10,5120]{1,0:T(8,128)(2,1)}, bf16[10,5120]{1,0:T(8,128)(2,1)S(1)}, u32[]{:S(2)}, u32[]{:S(2)}) collective-permute-start(bf16[10,5120]{1,0:T(8,128)(2,1)} %bitcast.1), channel_id=1, source_target_pairs={{0,128},{128,0},{1,129},{129,1},{2,130},{130,2},{3,131},{131,3},{4... | collective-permute-start | bytes 307208 | tf_op jit(solution)/shard_map/ppermute | solution.py:365
  6.2 13.5 %all-to-all-start = ((f32[32,4,128]{2,1,0:T(4,128)}), f32[32,4,128]{2,1,0:T(4,128)S(1)}, u32[]{:S(2)}, u32[]{:S(2)}) async-start(f32[32,4,128]{2,1,0:T(4,128)} %route_hidden.1), calls=%async_computation | async-start | bytes 131072 | tf_op jit(solution)/shard_map/all_to_all | solution.py:364
  19.7 2.1 %collective-permute-start.1 = (bf16[10,5120]{1,0:T(8,128)(2,1)}, bf16[10,5120]{1,0:T(8,128)(2,1)S(1)}, u32[]{:S(2)}, u32[]{:S(2)}) collective-permute-start(bf16[10,5120]{1,0:T(8,128)(2,1)} %bitcast.2), channel_id=1, source_target_pairs={{0,1},{1,0},{2,3},{3,2},{4,5},{5,4},{6,7},{7,6},{8,9},{9,8},{10,11... | collective-permute-start | bytes 307208 | tf_op jit(solution)/shard_map/ppermute | solution.py:344
  21.9 2.2 %collective-permute-start.2 = (bf16[10,5120]{1,0:T(8,128)(2,1)S(1)}, bf16[10,5120]{1,0:T(8,128)(2,1)S(1)}, u32[]{:S(2)}, u32[]{:S(2)}) collective-permute-start(bf16[10,5120]{1,0:T(8,128)(2,1)S(1)} %collective-permute-done.pair_rows), channel_id=1, source_target_pairs={{0,1},{1,0},{2,3},{3,2},{4,5},{5,4},{6,7},{7,6},{8,9},{9,8},{10,11... | collective-permute-start | bytes 307208 | tf_op jit(solution)/shard_map/ppermute | solution.py:344
  24.0 0.0 copy-start
  24.1 0.9 %copy-done = bf16[1,10,5120]{2,1,0:T(8,128)(2,1)S(1)} copy-done((bf16[1,10,5120]{2,1,0:T(8,128)(2,1)S(1)}, bf16[1,10,5120]{2,1,0:T(8,128)(2,1)}, u32[]{:S(2)}) %copy-start) | copy-done | bytes 102424
  25.0 3.9 %all-to-all-done.hidden = f32[32,4,128]{2,1,0:T(4,128)S(1)} async-done(((f32[32,4,128]{2,1,0:T(4,128)}), f32[32,4,128]{2,1,0:T(4,128)S(1)}, u32[]{:S(2)}, u32[]{:S(2)}) %all-to-all-start) | async-done | bytes 65568 | tf_op jit(solution)/shard_map/all_to_all | solution.py:364
  28.9 1.1 %project.1 = bf16[16,40,128]{2,1,0:T(8,128)(2,1)} custom-call(f32[32,4,128]{2,1,0:T(4,128)S(1)} %all-to-all-done.hidden, bf16[32,5120]{1,0:T(8,128)(2,1)S(1)} %pack_rows.1.near_rows, bf16[10,5120]{1,0:T(8,128)(2,1)S(1)} %collective-permute-done.1.far_rows, bf16[10,5120]{1,0:T(8,128)(2,1)S(1)} %collective-permute-done.2.far_pair), custom_call_target="tpu_custom_call" | custom-call | bytes 761856 | tf_op jit(solution)/shard_map/project/pallas_call | solution.py:331
  30.1 4.8 %all-to-all-start.1 = ((bf16[16,40,128]{2,1,0:T(8,128)(2,1)}), bf16[16,40,128]{2,1,0:T(8,128)(2,1)S(1)}, u32[]{:S(2)}, u32[]{:S(2)}) async-start(bf16[16,40,128]{2,1,0:T(8,128)(2,1)} %project.1), calls=%async_computation.1 | async-start | bytes 327680 | tf_op jit(solution)/shard_map/all_to_all | solution.py:388
  34.9 0.0 copy-start.1
  34.9 0.0 copy-start.2
  34.9 0.0 copy-start.4
  34.9 2.5 %fetch_cache.1 = (bf16[1024,512]{1,0:T(8,128)(2,1)S(1)}, bf16[2,1024,512]{2,1,0:T(8,128)(2,1)}) custom-call(bf16[2,2,1024,512]{3,2,1,0:T(8,128)(2,1)} %cache.1), custom_call_target="tpu_custom_call" | custom-call | tf_op jit(solution)/shard_map/fetch_cache/pallas_call | solution.py:390
  37.4 2.4 %collective-permute-start.3 = (bf16[2,1024,512]{2,1,0:T(8,128)(2,1)}, bf16[2,1024,512]{2,1,0:T(8,128)(2,1)S(1)}, u32[]{:S(2)}, u32[]{:S(2)}) collective-permute-start(bf16[2,1024,512]{2,1,0:T(8,128)(2,1)} %get-tuple-element.42), channel_id=1, source_target_pairs={{0,1},{1,0},{2,3},{3,2},{4,5},{5,4},{6,7},{7,6},{8,9},{9,8},{10,11... | collective-permute-start | bytes 6291464 | tf_op jit(solution)/shard_map/ppermute | solution.py:344
  39.8 0.6 prepare_rows.1
  40.4 4.8 %all-to-all-done.1.received = bf16[16,40,128]{2,1,0:T(8,128)(2,1)S(1)} async-done(((bf16[16,40,128]{2,1,0:T(8,128)(2,1)}), bf16[16,40,128]{2,1,0:T(8,128)(2,1)S(1)}, u32[]{:S(2)}, u32[]{:S(2)}) %all-to-all-start.1) | async-done | bytes 163872 | tf_op jit(solution)/shard_map/all_to_all | solution.py:388
  45.2 13.7 %all_to_all.20.shares = bf16[8,40,128]{2,1,0:T(8,128)(2,1)S(1)} all-to-all(bf16[8,40,128]{2,1,0:T(8,128)(2,1)S(1)} %sum_over_replicas.1), channel_id=1, replica_groups=mesh['yp'=2,'yq'=2,'z'=8,'yh'=2,'x'=4,'core'=2] {'yh','x'}, dimensions={0} | all-to-all | bytes 163840 | tf_op jit(solution)/shard_map/all_to_all | solution.py:429
  58.9 1.5 %both_steps.1 = (bf16[8,72,128]{2,1,0:T(8,128)(2,1)S(1)}, bf16[8,128]{1,0:T(8,128)(2,1)S(1)}) custom-call(s32[1,128]{1,0:T(1,128)S(1)} %get-tuple-element.36.length, bf16[8,40,128]{2,1,0:T(8,128)(2,1)S(1)} %all_to_all.20.shares, f32[1,128]{1,0:T(1,128)S(1)} %get-tuple-element.38.cosine, f32[1,128]{1,0:T(1,128)S(1)} %get-tuple-element.39.sine, ...), custom_call_target="tpu_custom_call" | custom-call | bytes 7583232 | tf_op jit(solution)/shard_map/both_steps/pallas_call | solution.py:331
  60.4 11.9 %all_to_all.21.shares = bf16[8,72,128]{2,1,0:T(8,128)(2,1)S(1)} all-to-all(bf16[8,72,128]{2,1,0:T(8,128)(2,1)S(1)} %get-tuple-element.44), channel_id=1, replica_groups=mesh['yp'=2,'yq'=2,'z'=8,'yh'=2,'x'=4,'core'=2] {'yh','x'}, dimensions={0} | all-to-all | bytes 294912 | tf_op jit(solution)/shard_map/all_to_all | solution.py:444
  72.3 0.2 combine.1.mine
  72.5 7.7 %collective-permute-start.4 = (bf16[72,128]{1,0:T(8,128)(2,1)S(1)}, bf16[72,128]{1,0:T(8,128)(2,1)S(1)}, u32[]{:S(2)}, u32[]{:S(2)}) collective-permute-start(bf16[72,128]{1,0:T(8,128)(2,1)S(1)} %combine.1.mine), channel_id=1, source_target_pairs={{0,1},{1,0},{2,3},{3,2},{4,5},{5,4},{6,7},{7,6},{8,9},{9,8},{10,11... | collective-permute-start | bytes 55304 | tf_op jit(solution)/shard_map/ppermute | solution.py:344
  80.2 0.8 %collective-permute-done.4.theirs = bf16[72,128]{1,0:T(8,128)(2,1)S(1)} collective-permute-done((bf16[72,128]{1,0:T(8,128)(2,1)S(1)}, bf16[72,128]{1,0:T(8,128)(2,1)S(1)}, u32[]{:S(2)}, u32[]{:S(2)}) %collective-permute-start.4) | collective-permute-done | bytes 18464 | tf_op jit(solution)/shard_map/ppermute | solution.py:344
  81.0 0.7 assemble.1
  (11 shorter events, 0.1 us)
Async XLA Ops:
  2.2 19.7 %collective-permute-start = (bf16[10,5120]{1,0:T(8,128)(2,1)}, bf16[10,5120]{1,0:T(8,128)(2,1)S(1)}, u32[]{:S(2)}, u32[]{:S(2)}) collective-permute-start(bf16[10,5120]{1,0:T(8,128)(2,1)} %bitcast.1), channel_id=1, source_target_pairs={{0,128},{128,0},{1,129},{129,1},{2,130},{130,2},{3,131},{131,3},{4... | collective-permute-start | bytes 307208 | tf_op jit(solution)/shard_map/ppermute | solution.py:365
  6.2 22.7 %all-to-all-start = ((f32[32,4,128]{2,1,0:T(4,128)}), f32[32,4,128]{2,1,0:T(4,128)S(1)}, u32[]{:S(2)}, u32[]{:S(2)}) async-start(f32[32,4,128]{2,1,0:T(4,128)} %route_hidden.1), calls=%async_computation | async-start | bytes 131072 | tf_op jit(solution)/shard_map/all_to_all | solution.py:364
  19.7 5.3 %collective-permute-start.1 = (bf16[10,5120]{1,0:T(8,128)(2,1)}, bf16[10,5120]{1,0:T(8,128)(2,1)S(1)}, u32[]{:S(2)}, u32[]{:S(2)}) collective-permute-start(bf16[10,5120]{1,0:T(8,128)(2,1)} %bitcast.2), channel_id=1, source_target_pairs={{0,1},{1,0},{2,3},{3,2},{4,5},{5,4},{6,7},{7,6},{8,9},{9,8},{10,11... | collective-permute-start | bytes 307208 | tf_op jit(solution)/shard_map/ppermute | solution.py:344
  21.9 7.1 %collective-permute-start.2 = (bf16[10,5120]{1,0:T(8,128)(2,1)S(1)}, bf16[10,5120]{1,0:T(8,128)(2,1)S(1)}, u32[]{:S(2)}, u32[]{:S(2)}) collective-permute-start(bf16[10,5120]{1,0:T(8,128)(2,1)S(1)} %collective-permute-done.pair_rows), channel_id=1, source_target_pairs={{0,1},{1,0},{2,3},{3,2},{4,5},{5,4},{6,7},{7,6},{8,9},{9,8},{10,11... | collective-permute-start | bytes 307208 | tf_op jit(solution)/shard_map/ppermute | solution.py:344
  24.0 0.9 %copy-start = (bf16[1,10,5120]{2,1,0:T(8,128)(2,1)S(1)}, bf16[1,10,5120]{2,1,0:T(8,128)(2,1)}, u32[]{:S(2)}) copy-start(bf16[1,10,5120]{2,1,0:T(8,128)(2,1)} %param.13) | copy-start | bytes 307204
  30.1 15.1 %all-to-all-start.1 = ((bf16[16,40,128]{2,1,0:T(8,128)(2,1)}), bf16[16,40,128]{2,1,0:T(8,128)(2,1)S(1)}, u32[]{:S(2)}, u32[]{:S(2)}) async-start(bf16[16,40,128]{2,1,0:T(8,128)(2,1)} %project.1), calls=%async_computation.1 | async-start | bytes 327680 | tf_op jit(solution)/shard_map/all_to_all | solution.py:388
  34.9 4.9 %copy-start.1 = (bf16[2,4096]{1,0:T(2,128)(2,1)S(1)}, bf16[2,4096]{1,0:T(2,128)(2,1)}, u32[]{:S(2)}) copy-start(bf16[2,4096]{1,0:T(2,128)(2,1)} %queries.1) | copy-start | bytes 49156
  34.9 4.9 %copy-start.2 = (bf16[2,1024]{1,0:T(2,128)(2,1)S(1)}, bf16[2,1024]{1,0:T(2,128)(2,1)}, u32[]{:S(2)}) copy-start(bf16[2,1024]{1,0:T(2,128)(2,1)} %fresh.1) | copy-start | bytes 12292
  34.9 4.9 %copy-start.3 = (s32[2]{0:T(128)S(1)}, s32[2]{0:T(128)}, u32[]{:S(2)}) copy-start(s32[2]{0:T(128)} %lengths) | copy-start | bytes 28
  34.9 4.9 %copy-start.4 = (f32[1,128]{1,0:T(1,128)S(1)}, f32[1,128]{1,0:T(1,128)}, u32[]{:S(2)}) copy-start(f32[1,128]{1,0:T(1,128)} %constant.2.clone.frequency) | copy-start | bytes 1540
  37.4 21.5 %collective-permute-start.3 = (bf16[2,1024,512]{2,1,0:T(8,128)(2,1)}, bf16[2,1024,512]{2,1,0:T(8,128)(2,1)S(1)}, u32[]{:S(2)}, u32[]{:S(2)}) collective-permute-start(bf16[2,1024,512]{2,1,0:T(8,128)(2,1)} %get-tuple-element.42), channel_id=1, source_target_pairs={{0,1},{1,0},{2,3},{3,2},{4,5},{5,4},{6,7},{7,6},{8,9},{9,8},{10,11... | collective-permute-start | bytes 6291464 | tf_op jit(solution)/shard_map/ppermute | solution.py:344
  72.5 8.5 %collective-permute-start.4 = (bf16[72,128]{1,0:T(8,128)(2,1)S(1)}, bf16[72,128]{1,0:T(8,128)(2,1)S(1)}, u32[]{:S(2)}, u32[]{:S(2)}) collective-permute-start(bf16[72,128]{1,0:T(8,128)(2,1)S(1)} %combine.1.mine), channel_id=1, source_target_pairs={{0,1},{1,0},{2,3},{3,2},{4,5},{5,4},{6,7},{7,6},{8,9},{9,8},{10,11... | collective-permute-start | bytes 55304 | tf_op jit(solution)/shard_map/ppermute | solution.py:344

commit v7 on v6

--- a/solution.py
+++ b/solution.py
@@ -12,7 +12,7 @@
 GROUP = QH // KVH
 HEADS = QH + 2 * KVH
 REP = ("yp", "yq", "z")
-FOLD = ("yp", "z")
+FOLD = ("yq", "z")
 CHIPS = ("yh", "x")
 CTX = ("yh", "x", "core")
 MASKED = -3e38
@@ -164,7 +164,7 @@
         for outer in range(2):
             first = (2 * core + outer) * column_size
             for pair in range(2):
-                block = (2 * outer + pair) * column_size
+                block = (2 * pair + outer) * column_size
                 out[first : first + column_size, pair, :] = folded[block : block + column_size]
 
 
@@ -177,7 +177,7 @@
 
 def project_kernel(hidden, near_rows, far_rows, far_pair, out, rows, wide):
     core = lax.axis_index("core")
-    side = lax.axis_index("yq")
+    side = lax.axis_index("yp")
     bucket_rows = far_rows.shape[0]
     slots = out.shape[0]
     rows[...] = jnp.zeros_like(rows)
@@ -362,7 +362,7 @@
     )
     by_slot, sectioned, kv_cache = lax.optimization_barrier((by_slot, sectioned, kv_cache))
     hidden = lax.all_to_all(by_slot, ("core",) + FOLD, 0, 0, tiled=True)
-    pair_rows = lax.ppermute(sectioned[0], "yq", [(0, 1), (1, 0)])
+    pair_rows = lax.ppermute(sectioned[0], "yp", [(0, 1), (1, 0)])
     far_rows = swap(sectioned[0])
     far_pair = swap(pair_rows)
     (near_rows,) = kernel_call(

time: 82.2 us -> 79.4 us (0.966)
  waiting for transfers between devices: 9.52 us -> 5.52 us
  blocking collectives: 25.6 us -> 27.6 us
  starting transfers between devices: 36.7 us -> 35.8 us
    all_to_all x1, waiting for transfers between devices: 4.76 us -> 2.06 us  [local(): received = lax.all_to_all(partial_sum, FOLD, 0, 0, tiled=True)]
    all_to_all x1, blocking collectives: 13.7 us -> 15.6 us  [local(): shares = lax.all_to_all(reduced, CHIPS, 0, 0, tiled=True)]
    all_to_all x1, waiting for transfers between devices: 3.93 us -> 2.63 us  [local(): hidden = lax.all_to_all(by_slot, ('core',) + FOLD, 0, 0, tiled=True)]
    ppermute x4, starting transfers between devices: 14.4 us -> 13.2 us  [swap(): return lax.ppermute(value, 'core', [(0, 1), (1, 0)])]
    ppermute x1, starting transfers between devices: 4.02 us -> 5.04 us  [local(): pair_rows = lax.ppermute(sectioned[0], 'yp', [(0, 1), (1, 0)])]
    all_to_all x1, starting transfers between devices: 13.5 us -> 12.5 us  [local(): hidden = lax.all_to_all(by_slot, ('core',) + FOLD, 0, 0, tiled=True)]
where the time goes in v7:
time: 79.4 us; the launch traced here: 78.8 us
  starting transfers between devices  35.8 us (45%)
  blocking collectives  27.6 us (35%)
  Pallas kernels  8.17 us (10%)
  waiting for transfers between devices  5.52 us (7%)
  local copies, waits for them, and re-layouts  0.94 us (1%)
  between operations  0.81 us (1%)
    all_to_all x1, blocking collectives, local(): shares = lax.all_to_all(reduced, CHIPS, 0, 0, tiled=True)  15.6 us
    ppermute x4, starting transfers between devices, swap(): return lax.ppermute(value, 'core', [(0, 1), (1, 0)])  13.2 us
    all_to_all x1, starting transfers between devices, local(): hidden = lax.all_to_all(by_slot, ('core',) + FOLD, 0, 0, tiled=True)  12.5 us
    all_to_all x1, blocking collectives, local(): gathered = lax.all_to_all(payload, CHIPS, 0, 0, tiled=True)  11.9 us
    pallas_call x8, Pallas kernels, kernel_call(): pl.pallas_call(kernel, in_specs=[pl.BlockSpec(memory_space=kinds[one]) fo...  5.7 us
    all_to_all x1, starting transfers between devices, local(): received = lax.all_to_all(partial_sum, FOLD, 0, 0, tiled=True)  5.19 us
    ppermute x1, starting transfers between devices, local(): pair_rows = lax.ppermute(sectioned[0], 'yp', [(0, 1), (1, 0)])  5.04 us
    all_to_all x1, waiting for transfers between devices, local(): hidden = lax.all_to_all(by_slot, ('core',) + FOLD, 0, 0, tiled=True)  2.63 us
  transfers between devices with their start and end apart: 7, of which 3 were waited for; matrix products, arithmetic and copies ran while one was open for 0% of the time, Pallas kernels for 4%

profile of v7, /device:TPU:1, one launch (start us, length us, event | category | flops | bytes accessed | tf_op | source)
XLA Modules:
  0.0 78.8 jit_solution(10932012039682208780)
XLA Ops:
  0.6 1.6 %route_hidden.1 = f32[32,4,128]{2,1,0:T(4,128)} custom-call(bf16[2,320]{1,0:T(2,128)(2,1)} %hidden.1, s32[1,32]{1,0:T(1,128)} %owners.1), custom_call_target="tpu_custom_call" | custom-call | bytes 66944 | tf_op jit(solution)/shard_map/route_hidden/pallas_call | solution.py:331
  2.2 5.0 %collective-permute-start = (bf16[10,5120]{1,0:T(8,128)(2,1)}, bf16[10,5120]{1,0:T(8,128)(2,1)S(1)}, u32[]{:S(2)}, u32[]{:S(2)}) collective-permute-start(bf16[10,5120]{1,0:T(8,128)(2,1)} %bitcast.1), channel_id=1, source_target_pairs={{0,256},{256,0},{1,257},{257,1},{2,258},{258,2},{3,259},{259,3},{4... | collective-permute-start | bytes 307208 | tf_op jit(solution)/shard_map/ppermute | solution.py:365
  7.2 12.5 %all-to-all-start = ((f32[32,4,128]{2,1,0:T(4,128)}), f32[32,4,128]{2,1,0:T(4,128)S(1)}, u32[]{:S(2)}, u32[]{:S(2)}) async-start(f32[32,4,128]{2,1,0:T(4,128)} %route_hidden.1), calls=%async_computation | async-start | bytes 131072 | tf_op jit(solution)/shard_map/all_to_all | solution.py:364
  19.7 2.1 %collective-permute-start.1 = (bf16[10,5120]{1,0:T(8,128)(2,1)}, bf16[10,5120]{1,0:T(8,128)(2,1)S(1)}, u32[]{:S(2)}, u32[]{:S(2)}) collective-permute-start(bf16[10,5120]{1,0:T(8,128)(2,1)} %bitcast.2), channel_id=1, source_target_pairs={{0,1},{1,0},{2,3},{3,2},{4,5},{5,4},{6,7},{7,6},{8,9},{9,8},{10,11... | collective-permute-start | bytes 307208 | tf_op jit(solution)/shard_map/ppermute | solution.py:344
  21.9 2.2 %collective-permute-start.2 = (bf16[10,5120]{1,0:T(8,128)(2,1)S(1)}, bf16[10,5120]{1,0:T(8,128)(2,1)S(1)}, u32[]{:S(2)}, u32[]{:S(2)}) collective-permute-start(bf16[10,5120]{1,0:T(8,128)(2,1)S(1)} %collective-permute-done.pair_rows), channel_id=1, source_target_pairs={{0,1},{1,0},{2,3},{3,2},{4,5},{5,4},{6,7},{7,6},{8,9},{9,8},{10,11... | collective-permute-start | bytes 307208 | tf_op jit(solution)/shard_map/ppermute | solution.py:344
  24.0 0.0 copy-start
  24.1 0.9 %copy-done = bf16[1,10,5120]{2,1,0:T(8,128)(2,1)S(1)} copy-done((bf16[1,10,5120]{2,1,0:T(8,128)(2,1)S(1)}, bf16[1,10,5120]{2,1,0:T(8,128)(2,1)}, u32[]{:S(2)}) %copy-start) | copy-done | bytes 102424
  25.0 2.6 %all-to-all-done.hidden = f32[32,4,128]{2,1,0:T(4,128)S(1)} async-done(((f32[32,4,128]{2,1,0:T(4,128)}), f32[32,4,128]{2,1,0:T(4,128)S(1)}, u32[]{:S(2)}, u32[]{:S(2)}) %all-to-all-start) | async-done | bytes 65568 | tf_op jit(solution)/shard_map/all_to_all | solution.py:364
  27.7 1.1 %project.1 = bf16[16,40,128]{2,1,0:T(8,128)(2,1)} custom-call(f32[32,4,128]{2,1,0:T(4,128)S(1)} %all-to-all-done.hidden, bf16[32,5120]{1,0:T(8,128)(2,1)S(1)} %pack_rows.1.near_rows, bf16[10,5120]{1,0:T(8,128)(2,1)S(1)} %collective-permute-done.1.far_rows, bf16[10,5120]{1,0:T(8,128)(2,1)S(1)} %collective-permute-done.2.far_pair), custom_call_target="tpu_custom_call" | custom-call | bytes 761856 | tf_op jit(solution)/shard_map/project/pallas_call | solution.py:331
  28.8 5.2 %all-to-all-start.1 = ((bf16[16,40,128]{2,1,0:T(8,128)(2,1)}), bf16[16,40,128]{2,1,0:T(8,128)(2,1)S(1)}, u32[]{:S(2)}, u32[]{:S(2)}) async-start(bf16[16,40,128]{2,1,0:T(8,128)(2,1)} %project.1), calls=%async_computation.1 | async-start | bytes 327680 | tf_op jit(solution)/shard_map/all_to_all | solution.py:388
  34.0 0.0 copy-start.1
  34.0 0.0 copy-start.2
  34.0 0.0 copy-start.4
  34.0 2.5 %fetch_cache.1 = (bf16[1024,512]{1,0:T(8,128)(2,1)S(1)}, bf16[2,1024,512]{2,1,0:T(8,128)(2,1)}) custom-call(bf16[2,2,1024,512]{3,2,1,0:T(8,128)(2,1)} %cache.1), custom_call_target="tpu_custom_call" | custom-call | tf_op jit(solution)/shard_map/fetch_cache/pallas_call | solution.py:390
  36.5 2.4 %collective-permute-start.3 = (bf16[2,1024,512]{2,1,0:T(8,128)(2,1)}, bf16[2,1024,512]{2,1,0:T(8,128)(2,1)S(1)}, u32[]{:S(2)}, u32[]{:S(2)}) collective-permute-start(bf16[2,1024,512]{2,1,0:T(8,128)(2,1)} %get-tuple-element.42), channel_id=1, source_target_pairs={{0,1},{1,0},{2,3},{3,2},{4,5},{5,4},{6,7},{7,6},{8,9},{9,8},{10,11... | collective-permute-start | bytes 6291464 | tf_op jit(solution)/shard_map/ppermute | solution.py:344
  38.9 0.6 prepare_rows.1
  39.5 2.1 %all-to-all-done.1.received = bf16[16,40,128]{2,1,0:T(8,128)(2,1)S(1)} async-done(((bf16[16,40,128]{2,1,0:T(8,128)(2,1)}), bf16[16,40,128]{2,1,0:T(8,128)(2,1)S(1)}, u32[]{:S(2)}, u32[]{:S(2)}) %all-to-all-start.1) | async-done | bytes 163872 | tf_op jit(solution)/shard_map/all_to_all | solution.py:388
  41.6 15.6 %all_to_all.20.shares = bf16[8,40,128]{2,1,0:T(8,128)(2,1)S(1)} all-to-all(bf16[8,40,128]{2,1,0:T(8,128)(2,1)S(1)} %sum_over_replicas.1), channel_id=1, replica_groups=mesh['yp'=2,'yq'=2,'z'=8,'yh'=2,'x'=4,'core'=2] {'yh','x'}, dimensions={0} | all-to-all | bytes 163840 | tf_op jit(solution)/shard_map/all_to_all | solution.py:429
  57.2 1.5 %both_steps.1 = (bf16[8,72,128]{2,1,0:T(8,128)(2,1)S(1)}, bf16[8,128]{1,0:T(8,128)(2,1)S(1)}) custom-call(s32[1,128]{1,0:T(1,128)S(1)} %get-tuple-element.36.length, bf16[8,40,128]{2,1,0:T(8,128)(2,1)S(1)} %all_to_all.20.shares, f32[1,128]{1,0:T(1,128)S(1)} %get-tuple-element.38.cosine, f32[1,128]{1,0:T(1,128)S(1)} %get-tuple-element.39.sine, ...), custom_call_target="tpu_custom_call" | custom-call | bytes 7583232 | tf_op jit(solution)/shard_map/both_steps/pallas_call | solution.py:331
  58.7 11.9 %all_to_all.21.shares = bf16[8,72,128]{2,1,0:T(8,128)(2,1)S(1)} all-to-all(bf16[8,72,128]{2,1,0:T(8,128)(2,1)S(1)} %get-tuple-element.44), channel_id=1, replica_groups=mesh['yp'=2,'yq'=2,'z'=8,'yh'=2,'x'=4,'core'=2] {'yh','x'}, dimensions={0} | all-to-all | bytes 294912 | tf_op jit(solution)/shard_map/all_to_all | solution.py:444
  70.7 0.2 combine.1.mine
  70.9 6.5 %collective-permute-start.4 = (bf16[72,128]{1,0:T(8,128)(2,1)S(1)}, bf16[72,128]{1,0:T(8,128)(2,1)S(1)}, u32[]{:S(2)}, u32[]{:S(2)}) collective-permute-start(bf16[72,128]{1,0:T(8,128)(2,1)S(1)} %combine.1.mine), channel_id=1, source_target_pairs={{0,1},{1,0},{2,3},{3,2},{4,5},{5,4},{6,7},{7,6},{8,9},{9,8},{10,11... | collective-permute-start | bytes 55304 | tf_op jit(solution)/shard_map/ppermute | solution.py:344
  77.4 0.8 %collective-permute-done.4.theirs = bf16[72,128]{1,0:T(8,128)(2,1)S(1)} collective-permute-done((bf16[72,128]{1,0:T(8,128)(2,1)S(1)}, bf16[72,128]{1,0:T(8,128)(2,1)S(1)}, u32[]{:S(2)}, u32[]{:S(2)}) %collective-permute-start.4) | collective-permute-done | bytes 18464 | tf_op jit(solution)/shard_map/ppermute | solution.py:344
  78.2 0.7 assemble.1
  (11 shorter events, 0.1 us)
Async XLA Ops:
  2.2 19.7 %collective-permute-start = (bf16[10,5120]{1,0:T(8,128)(2,1)}, bf16[10,5120]{1,0:T(8,128)(2,1)S(1)}, u32[]{:S(2)}, u32[]{:S(2)}) collective-permute-start(bf16[10,5120]{1,0:T(8,128)(2,1)} %bitcast.1), channel_id=1, source_target_pairs={{0,256},{256,0},{1,257},{257,1},{2,258},{258,2},{3,259},{259,3},{4... | collective-permute-start | bytes 307208 | tf_op jit(solution)/shard_map/ppermute | solution.py:365
  7.2 20.4 %all-to-all-start = ((f32[32,4,128]{2,1,0:T(4,128)}), f32[32,4,128]{2,1,0:T(4,128)S(1)}, u32[]{:S(2)}, u32[]{:S(2)}) async-start(f32[32,4,128]{2,1,0:T(4,128)} %route_hidden.1), calls=%async_computation | async-start | bytes 131072 | tf_op jit(solution)/shard_map/all_to_all | solution.py:364
  19.7 5.3 %collective-permute-start.1 = (bf16[10,5120]{1,0:T(8,128)(2,1)}, bf16[10,5120]{1,0:T(8,128)(2,1)S(1)}, u32[]{:S(2)}, u32[]{:S(2)}) collective-permute-start(bf16[10,5120]{1,0:T(8,128)(2,1)} %bitcast.2), channel_id=1, source_target_pairs={{0,1},{1,0},{2,3},{3,2},{4,5},{5,4},{6,7},{7,6},{8,9},{9,8},{10,11... | collective-permute-start | bytes 307208 | tf_op jit(solution)/shard_map/ppermute | solution.py:344
  21.9 5.8 %collective-permute-start.2 = (bf16[10,5120]{1,0:T(8,128)(2,1)S(1)}, bf16[10,5120]{1,0:T(8,128)(2,1)S(1)}, u32[]{:S(2)}, u32[]{:S(2)}) collective-permute-start(bf16[10,5120]{1,0:T(8,128)(2,1)S(1)} %collective-permute-done.pair_rows), channel_id=1, source_target_pairs={{0,1},{1,0},{2,3},{3,2},{4,5},{5,4},{6,7},{7,6},{8,9},{9,8},{10,11... | collective-permute-start | bytes 307208 | tf_op jit(solution)/shard_map/ppermute | solution.py:344
  24.0 0.9 %copy-start = (bf16[1,10,5120]{2,1,0:T(8,128)(2,1)S(1)}, bf16[1,10,5120]{2,1,0:T(8,128)(2,1)}, u32[]{:S(2)}) copy-start(bf16[1,10,5120]{2,1,0:T(8,128)(2,1)} %param.13) | copy-start | bytes 307204
  28.8 12.8 %all-to-all-start.1 = ((bf16[16,40,128]{2,1,0:T(8,128)(2,1)}), bf16[16,40,128]{2,1,0:T(8,128)(2,1)S(1)}, u32[]{:S(2)}, u32[]{:S(2)}) async-start(bf16[16,40,128]{2,1,0:T(8,128)(2,1)} %project.1), calls=%async_computation.1 | async-start | bytes 327680 | tf_op jit(solution)/shard_map/all_to_all | solution.py:388
  34.0 4.9 %copy-start.1 = (bf16[2,4096]{1,0:T(2,128)(2,1)S(1)}, bf16[2,4096]{1,0:T(2,128)(2,1)}, u32[]{:S(2)}) copy-start(bf16[2,4096]{1,0:T(2,128)(2,1)} %queries.1) | copy-start | bytes 49156
  34.0 4.9 %copy-start.2 = (bf16[2,1024]{1,0:T(2,128)(2,1)S(1)}, bf16[2,1024]{1,0:T(2,128)(2,1)}, u32[]{:S(2)}) copy-start(bf16[2,1024]{1,0:T(2,128)(2,1)} %fresh.1) | copy-start | bytes 12292
  34.0 4.9 %copy-start.3 = (s32[2]{0:T(128)S(1)}, s32[2]{0:T(128)}, u32[]{:S(2)}) copy-start(s32[2]{0:T(128)} %lengths) | copy-start | bytes 28
  34.0 4.9 %copy-start.4 = (f32[1,128]{1,0:T(1,128)S(1)}, f32[1,128]{1,0:T(1,128)}, u32[]{:S(2)}) copy-start(f32[1,128]{1,0:T(1,128)} %constant.2.clone.frequency) | copy-start | bytes 1540
  36.5 20.7 %collective-permute-start.3 = (bf16[2,1024,512]{2,1,0:T(8,128)(2,1)}, bf16[2,1024,512]{2,1,0:T(8,128)(2,1)S(1)}, u32[]{:S(2)}, u32[]{:S(2)}) collective-permute-start(bf16[2,1024,512]{2,1,0:T(8,128)(2,1)} %get-tuple-element.42), channel_id=1, source_target_pairs={{0,1},{1,0},{2,3},{3,2},{4,5},{5,4},{6,7},{7,6},{8,9},{9,8},{10,11... | collective-permute-start | bytes 6291464 | tf_op jit(solution)/shard_map/ppermute | solution.py:344
  70.9 7.3 %collective-permute-start.4 = (bf16[72,128]{1,0:T(8,128)(2,1)S(1)}, bf16[72,128]{1,0:T(8,128)(2,1)S(1)}, u32[]{:S(2)}, u32[]{:S(2)}) collective-permute-start(bf16[72,128]{1,0:T(8,128)(2,1)S(1)} %combine.1.mine), channel_id=1, source_target_pairs={{0,1},{1,0},{2,3},{3,2},{4,5},{5,4},{6,7},{7,6},{8,9},{9,8},{10,11... | collective-permute-start | bytes 55304 | tf_op jit(solution)/shard_map/ppermute | solution.py:344
